TPU v7x, 256 devices: a whole 4x4x8 slice. The times are simulated.
256 devices in a mesh: grp: 8 (over x, z_hi), seq: 32 (over y, z_lo, core).
Axes of the slice: x: 4, y: 4, z: 8 (z_hi: 2, z_lo: 4; z = z_hi * 4 + z_lo), core: 2. Of those that a mesh axis runs over, the one named last changes fastest.
Arguments:
- query: bfloat16 [65536, 4096], P(('grp', 'seq')), may hold values from -200 to 200
- comp_key: bfloat16 [65536, 512], P(('grp', 'seq')), may hold values from -6 to 6
- comp_value: bfloat16 [65536, 512], P(('grp', 'seq')), may hold values from -6 to 6
- out_grad: bfloat16 [65536, 4096], P(('grp', 'seq')), may hold values from -6 to 6
- prompt_key: bfloat16 [4096, 512], P(('grp', 'seq')), may hold values from -6 to 6
- prompt_value: bfloat16 [4096, 512], P(('grp', 'seq')), may hold values from -6 to 6
- prompt_len: int32 [32], P('grp'), may hold values from 32 to 128, as said below
- comp_len: int32 [512], P(('grp', 'seq')), may hold values from 1 to 128, as said below
- comp_group: int32 [512], P(('grp', 'seq')), may hold values from 0 to 3, as said below
Outputs:
- query_grad: bfloat16 [65536, 4096], P(('grp', 'seq'))
- comp_key_grad: bfloat16 [65536, 512], P(('grp', 'seq'))
- comp_value_grad: bfloat16 [65536, 512], P(('grp', 'seq'))
- prompt_key_grad: bfloat16 [4096, 512], P(('grp', 'seq'))
- prompt_value_grad: bfloat16 [4096, 512], P(('grp', 'seq'))
Inputs may be any that keep to these rules, and one draw needn't show every extreme that they name: `comp_len`: some completion has exactly 128 live tokens. `prompt_len`: some prompt has exactly 128 live tokens. `comp_group`: along each index of grp, every group has exactly 16 completions, on consecutive completions of the row taken cyclically, and the groups follow one another in rising order.
All inputs are finite; a program needn't handle non-finite values.
Results may differ from a plain program's by a relative error of at most 0.012.
Values may be sent and summed in bfloat16 or wider, within the bound.
No kernel may reach another device: no remote copies, remote signals or barrier semaphores. Data moves between devices by JAX's collectives and lax.ppermute only.
A program may use at most 128 MiB of HBM per device.

v0:
```python
import jax
import jax.numpy as jnp
from jax import lax
from jax.sharding import PartitionSpec as P

HD = 128


def slot_grads(q_rows, grad_rows, key_rows, value_rows, live_mask, first_key):
    query_count = q_rows.shape[0]
    key_count = key_rows.shape[0]
    groups = key_rows.shape[1] // HD
    repeat = q_rows.shape[1] // key_rows.shape[1]
    scaling = HD ** (-0.5)
    query_heads = q_rows.reshape(query_count, groups, repeat, HD)
    grad_heads = grad_rows.reshape(query_count, groups, repeat, HD)
    key_heads = key_rows.reshape(key_count, groups, HD)
    value_heads = value_rows.reshape(key_count, groups, HD)
    scores = (
        jnp.einsum("cgrd,lgd->grcl", query_heads, key_heads, preferred_element_type=jnp.float32)
        * scaling
    )
    scores = jnp.where(live_mask[None, None], scores, -1e30)
    row_max = jnp.max(scores, axis=-1, keepdims=True)
    lifted = jnp.exp(scores - row_max)
    row_sum = jnp.sum(lifted, axis=-1, keepdims=True)
    probability = lifted / row_sum
    weights_b = probability.astype(jnp.bfloat16)
    output = jnp.einsum(
        "grcl,lgd->cgrd", weights_b, value_heads, preferred_element_type=jnp.float32
    )
    row_delta = jnp.sum(grad_heads.astype(jnp.float32) * output, axis=-1)
    delta_cols = jnp.transpose(row_delta, (1, 2, 0))[..., None]
    prob_grad = jnp.einsum(
        "cgrd,lgd->grcl", grad_heads, value_heads, preferred_element_type=jnp.float32
    )
    score_b = (probability * (prob_grad - delta_cols)).astype(jnp.bfloat16)
    query_part = (
        jnp.einsum("grcl,lgd->cgrd", score_b, key_heads, preferred_element_type=jnp.float32)
        * scaling
    )
    key_part = (
        jnp.einsum("grcl,cgrd->lgd", score_b, query_heads, preferred_element_type=jnp.float32)
        * scaling
    )
    value_part = jnp.einsum(
        "grcl,cgrd->lgd", weights_b, grad_heads, preferred_element_type=jnp.float32
    )
    kept = key_count - first_key
    return (
        query_part.reshape(query_count, -1),
        key_part.reshape(kept, -1),
        value_part.reshape(kept, -1),
        row_max,
        row_sum,
        delta_cols,
    )


def on_device(
    query,
    comp_key,
    comp_value,
    out_grad,
    prompt_key,
    prompt_value,
    prompt_len,
    comp_len,
    comp_group,
):
    comp_count = comp_len.shape[0]
    row_count = query.shape[0]
    length = row_count // comp_count
    group_count = prompt_len.shape[0]
    kv_width = prompt_key.shape[1]
    seq_count = lax.axis_size("seq")
    live_total = lax.psum(jnp.sum(comp_len.astype(jnp.float32)), ("grp", "seq"))
    token_weight = jnp.float32(lax.axis_size("grp") * seq_count * row_count) / live_total
    row_keys, row_values = (
        lax.all_gather(prompt_key, "seq", axis=0, tiled=True),
        lax.all_gather(prompt_value, "seq", axis=0, tiled=True),
    )
    prompt_rows = row_keys.shape[0] // group_count
    member = comp_group[:, None] == jnp.arange(group_count, dtype=jnp.int32)[None, :]
    near_lens = jnp.sum(jnp.where(member, prompt_len[None, :], 0), axis=1)
    near_keys = jnp.stack(
        [
            lax.dynamic_slice_in_dim(row_keys, comp_group[slot] * prompt_rows, prompt_rows, 0)
            for slot in range(comp_count)
        ]
    )
    near_values = jnp.stack(
        [
            lax.dynamic_slice_in_dim(row_values, comp_group[slot] * prompt_rows, prompt_rows, 0)
            for slot in range(comp_count)
        ]
    )
    position = jnp.arange(length, dtype=jnp.int32)
    prompt_pos = jnp.arange(prompt_rows, dtype=jnp.int32)
    causal = position[None, :] <= position[:, None]
    q_slots = query.reshape(comp_count, length, -1)
    grad_slots = out_grad.reshape(comp_count, length, -1)
    live_rows = position[None, :] < comp_len[:, None]
    grad_slots = jnp.where(live_rows[:, :, None], grad_slots, jnp.zeros_like(grad_slots))
    key_slots = jnp.concatenate([near_keys, comp_key.reshape(comp_count, length, -1)], 1)
    value_slots = jnp.concatenate([near_values, comp_value.reshape(comp_count, length, -1)], 1)
    first_key = 0

    def one_slot(slot_items):
        q_rows, grad_rows, key_rows, value_rows, near_len = slot_items
        prompt_live = jnp.broadcast_to((prompt_pos < near_len)[None, :], (length, prompt_rows))
        live_mask = jnp.concatenate([prompt_live, causal], 1)
        return slot_grads(q_rows, grad_rows, key_rows, value_rows, live_mask, first_key)

    query_part, key_part, value_part, row_max, row_sum, delta_cols = lax.map(
        one_slot, (q_slots, grad_slots, key_slots, value_slots, near_lens)
    )
    own_start = prompt_rows - first_key
    query_grad = (query_part * token_weight).astype(jnp.bfloat16).reshape(row_count, -1)
    comp_key_grad = (
        (key_part[:, own_start:] * token_weight).astype(jnp.bfloat16).reshape(row_count, -1)
    )
    comp_value_grad = (
        (value_part[:, own_start:] * token_weight).astype(jnp.bfloat16).reshape(row_count, -1)
    )
    buffer_key = jnp.zeros((group_count * prompt_rows, kv_width), jnp.float32)
    buffer_value = jnp.zeros((group_count * prompt_rows, kv_width), jnp.float32)
    for slot in range(comp_count):
        start_row = comp_group[slot] * prompt_rows
        buffer_key = lax.dynamic_update_slice_in_dim(
            buffer_key,
            lax.dynamic_slice_in_dim(buffer_key, start_row, prompt_rows, 0)
            + key_part[slot, :prompt_rows],
            start_row,
            0,
        )
        buffer_value = lax.dynamic_update_slice_in_dim(
            buffer_value,
            lax.dynamic_slice_in_dim(buffer_value, start_row, prompt_rows, 0)
            + value_part[slot, :prompt_rows],
            start_row,
            0,
        )
    own_key, own_value = (
        lax.psum_scatter(buffer_key, "seq", scatter_dimension=0, tiled=True),
        lax.psum_scatter(buffer_value, "seq", scatter_dimension=0, tiled=True),
    )
    prompt_key_grad = (own_key * token_weight).astype(jnp.bfloat16)
    prompt_value_grad = (own_value * token_weight).astype(jnp.bfloat16)
    return (query_grad, comp_key_grad, comp_value_grad, prompt_key_grad, prompt_value_grad)


def solution(mesh):
    placed = (
        P(("grp", "seq"), None),
        P(("grp", "seq"), None),
        P(("grp", "seq"), None),
        P(("grp", "seq"), None),
        P(("grp", "seq"), None),
        P(("grp", "seq"), None),
        P("grp"),
        P(("grp", "seq")),
        P(("grp", "seq")),
    )
    return jax.shard_map(
        on_device,
        mesh=mesh,
        in_specs=placed,
        out_specs=(
            P(("grp", "seq"), None),
            P(("grp", "seq"), None),
            P(("grp", "seq"), None),
            P(("grp", "seq"), None),
            P(("grp", "seq"), None),
        ),
        check_vma=False,
    )
```

profile of v0, /device:TPU:4, one launch (start us, length us, event | category | flops | bytes accessed | tf_op | source)
XLA Modules:
  0.0 454.6 jit_solution(19631716638292466)
XLA Ops:
  7.2 1.3 fusion.26
  9.9 47.0 %all_gather.6 = bf16[512,512]{1,0:T(8,128)(2,1)S(1)} all-gather(bf16[16,512]{1,0:T(8,128)(2,1)} %param.15), channel_id=1, replica_groups=mesh['grp'=8,'seq'=32] {'seq'}, dimensions={0}, use_global_device_ids=true | all-gather | bytes 540672 | tf_op jit(solution)/shard_map/all_gather | solution.py:80
  56.9 40.2 %all_gather.7 = bf16[512,512]{1,0:T(8,128)(2,1)S(1)} all-gather(bf16[16,512]{1,0:T(8,128)(2,1)} %param.16), channel_id=1, replica_groups=mesh['grp'=8,'seq'=32] {'seq'}, dimensions={0}, use_global_device_ids=true | all-gather | bytes 540672 | tf_op jit(solution)/shard_map/all_gather | solution.py:81
  97.1 0.7 iota_compare_fusion.2
  97.8 0.9 fusion.24
  98.7 3.2 broadcast_select_fusion
  102.0 0.9 copy-done.15
  102.8 0.8 pad_maximum_fusion.1
  103.7 52.9 %while.15 = (s32[]{:T(128)}, f32[2,128,4096]{1,2,0:T(8,128)}, f32[2,256,512]{1,2,0:T(8,128)}, f32[2,256,512]{1,2,0:T(8,128)}, bf16[2,256,512]{2,1,0:T(8,128)(2,1...) while((s32[]{:T(128)}, f32[2,128,4096]{1,2,0:T(8,128)}, ...), condition=%wide.region_5.6_spmd.clone, body=%wide.region_1.5_spmd.clone.sunk | while | flops 1623372160 | bytes 90359480 | solution.py:115
  103.7 1.5 constant_dynamic-slice_fusion.11
  105.1 0.7 copy.114
  105.9 0.1 copy.111
  106.0 0.7 dynamic_slice.66
  106.7 0.6 iota_compare_fusion.6
  107.5 3.4 fusion.72
  110.9 2.9 fusion.73
  113.8 1.1 constant_dynamic-slice_fusion.10
  114.8 1.6 copy.113
  116.4 1.7 constant_dynamic-slice_fusion.9
  118.1 1.8 copy.112
  119.9 1.5 fusion.74
  121.5 3.1 fusion.75
  124.6 0.8 fusion.77
  125.5 0.8 fusion.76
  126.3 0.4 copy-done.8
  126.7 0.3 copy-done.12
  127.1 1.0 copy-done.9
  128.1 0.5 convolution_multiply_fusion.2
  128.6 1.5 constant_dynamic-update-slice_fusion.5
  130.1 1.5 constant_dynamic-slice_fusion.11
  131.6 0.7 copy.114
  132.3 0.1 copy.111
  132.5 0.7 dynamic_slice.66
  133.1 0.6 iota_compare_fusion.6
  133.9 3.4 fusion.72
  137.3 2.9 fusion.73
  140.2 1.1 constant_dynamic-slice_fusion.10
  141.3 1.6 copy.113
  142.9 1.7 constant_dynamic-slice_fusion.9
  144.6 1.8 copy.112
  146.4 1.5 fusion.74
  147.9 3.1 fusion.75
  151.1 0.8 fusion.77
  151.9 0.8 fusion.76
  152.7 0.4 copy-done.8
  153.1 0.3 copy-done.12
  153.6 1.0 copy-done.9
  154.6 0.5 convolution_multiply_fusion.2
  155.1 1.4 constant_dynamic-update-slice_fusion.5
  156.5 1.6 copy.85
  158.3 1.0 copy-done.7
  159.5 0.3 copy.83
  160.1 1.0 copy-done.6
  161.1 0.6 convert_reduce_fusion
  161.7 74.8 %psum.7 = f32[]{:T(128)} all-reduce(f32[]{:T(128)} %convert_reduce_fusion), channel_id=1, replica_groups=mesh['grp'=8,'seq'=32] {'grp','seq'}, use_global_device_ids=true, to_apply=%region_7.8 | all-reduce | flops 1 | bytes 8 | tf_op jit(solution)/shard_map/psum | solution.py:77
  237.1 2.5 multiply_convert_fusion
  239.7 2.7 copy.80
  242.4 0.9 copy.81
  243.3 1.1 multiply_convert_fusion.1
  244.4 0.9 copy.82
  245.2 57.0 %reduce-scatter.5.cloned.1.call-done = f32[16,512]{1,0:T(8,128)} async-done(((f32[512,512]{1,0:T(8,128)}), f32[16,512]{1,0:T(8,128)}) %reduce-scatter.5.cloned.1.call-update) | async-done | bytes 32784 | tf_op jit(solution)/shard_map/reduce_scatter | solution.py:146
  302.2 1.4 multiply_convert_fusion.3
  303.6 142.8 %reduce-scatter.3.cloned.1.call-done = f32[16,512]{1,0:T(8,128)} async-done(((f32[512,512]{1,0:T(8,128)}), f32[16,512]{1,0:T(8,128)}) %reduce-scatter.3.cloned.1.call-update) | async-done | bytes 32784 | tf_op jit(solution)/shard_map/reduce_scatter | solution.py:145
  446.3 1.4 multiply_convert_fusion.4
  (71 shorter events, 1.3 us)
Async XLA Ops:
  7.2 295.0 %reduce-scatter.5.cloned.1.call-start = ((), (), s32[]{:S(2)}) async-start(), calls=%async_computation.3 | async-start | bytes 1081344 | tf_op jit(solution)/shard_map/reduce_scatter | solution.py:146
  98.7 3.2 copy-start.14
  101.9 0.9 copy-start.15
  103.7 2.2 copy-start.4
  105.8 5.1 %copy-start = (bf16[1,128,4096]{1,2,0:T(8,128)(2,1)}, bf16[1,128,4096]{1,2,0:T(8,128)(2,1)S(1)}, u32[]{:S(2)}) copy-start(bf16[1,128,4096]{1,2,0:T(8,128)(2,1)S(1)} %copy.114) | copy-start | bytes 3145732 | tf_op jit(solution)/shard_map/while
  110.9 2.9 copy-start.3
  119.9 1.6 copy-start.2
  121.5 3.1 copy-start.1
  125.4 1.2 copy-start.8
  125.5 1.5 copy-start.12
  127.1 1.0 copy-start.9
  127.1 1.5 copy-start.13
  128.6 1.5 copy-start.5
  130.1 2.2 copy-start.4
  132.3 5.1 %copy-start = (bf16[1,128,4096]{1,2,0:T(8,128)(2,1)}, bf16[1,128,4096]{1,2,0:T(8,128)(2,1)S(1)}, u32[]{:S(2)}) copy-start(bf16[1,128,4096]{1,2,0:T(8,128)(2,1)S(1)} %copy.114) | copy-start | bytes 3145732 | tf_op jit(solution)/shard_map/while
  137.3 2.9 copy-start.3
  146.4 1.5 copy-start.2
  147.9 3.2 copy-start.1
  151.9 1.2 copy-start.8
  151.9 1.5 copy-start.12
  153.5 1.0 copy-start.9
  153.6 1.5 copy-start.13
  155.1 1.5 copy-start.5
  158.1 1.4 copy-start.10
  158.3 1.0 copy-start.7
  159.4 287.0 %reduce-scatter.3.cloned.1.call-start = ((), (), s32[]{:S(2)}) async-start(), calls=%async_computation.2 | async-start | bytes 1081344 | tf_op jit(solution)/shard_map/reduce_scatter | solution.py:145
  159.8 1.2 copy-start.16
  160.1 1.0 copy-start.6
  239.7 2.7 copy-start.11
Sparse Core Ops, SparseCore 0:
  159.5 142.6 reduce-scatter.4
  304.9 141.4 reduce-scatter.2
where the time goes:
time: 456 us; the launch traced here: 455 us
  waiting for transfers between devices  200 us (44%)
  blocking collectives  162 us (36%)
  local copies, waits for them, and re-layouts  35.8 us (8%)
  matrix products  20.3 us (4%)
  other arithmetic  20 us (4%)
  between operations  16.2 us (4%)
    reduce_scatter x1, waiting for transfers between devices, on_device(): lax.psum_scatter(buffer_key, 'seq', scatter_dimension=0, tiled=True)  143 us
    psum x1, blocking collectives, on_device(): live_total = lax.psum(jnp.sum(comp_len.astype(jnp.float32)), ('grp', 'seq'))  74.8 us
    reduce_scatter x1, waiting for transfers between devices, on_device(): lax.psum_scatter(buffer_value, 'seq', scatter_dimension=0, tiled=True)  57 us
    all_gather x1, blocking collectives, on_device(): lax.all_gather(prompt_key, 'seq', axis=0, tiled=True)  47 us
    all_gather x1, blocking collectives, on_device(): lax.all_gather(prompt_value, 'seq', axis=0, tiled=True)  40.2 us
    dynamic_slice x18, local copies, waits for them, and re-layouts, on_device(): lax.map(one_slot, (q_slots, grad_slots, key_slots, value_slots, near_lens))  18.2 us
  transfers between devices with their start and end apart: 2, of which 2 were waited for; matrix products, arithmetic and copies ran while one was open for 2% of the time, Pallas kernels for 0%

commit v1 on v0

v1 whole, which is shorter than its diff:
```python
import math

import jax
import jax.numpy as jnp
from jax import lax
from jax.experimental import pallas as pl
from jax.experimental.pallas import tpu as pltpu
from jax.sharding import PartitionSpec as P

HD = 128
CLEN = 128
PLEN = 128
COMP = 2
KVH = 4
REP = 8
KVW = KVH * HD
QW = REP * HD
GPR = 4
ROWS = 65536.0
SCALE = HD ** -0.5
EXP2_SCALE = SCALE * math.log2(math.e)
MASKED = -1e30
VMEM = pltpu.VMEM
F32 = jnp.float32
BF16 = jnp.bfloat16


def dot_nt(a, b):
    return lax.dot_general(a, b, (((1,), (1,)), ((), ())), preferred_element_type=F32)


def dot_nn(a, b):
    return lax.dot_general(a, b, (((1,), (0,)), ((), ())), preferred_element_type=F32)


def dot_tn(a, b):
    return lax.dot_general(a, b, (((0,), (0,)), ((), ())), preferred_element_type=F32)


def joined_dot(pairs):
    return dot_nn(
        jnp.concatenate([a for a, _ in pairs], 1), jnp.concatenate([b for _, b in pairs], 0)
    )


def position():
    place = lax.axis_index("seq")
    return place // 8, (place // 2) % 4, place % 2


def cols_of(kv, first=0):
    return slice(first + kv * HD, first + (kv + 1) * HD)


def heads_of(kv, pair):
    return [slice((kv * REP + 2 * pair + j) * HD, (kv * REP + 2 * pair + j + 1) * HD) for j in range(2)]


def pack_kernel(comp_len, comp_group, prompt_key, prompt_value, mine, lens, groups, sems):
    copies = [
        pltpu.make_async_copy(comp_len, lens, sems.at[0]),
        pltpu.make_async_copy(comp_group, groups, sems.at[1]),
        pltpu.make_async_copy(prompt_key, mine.at[:, pl.ds(0, KVW)], sems.at[2]),
        pltpu.make_async_copy(prompt_value, mine.at[:, pl.ds(KVW, KVW)], sems.at[3]),
    ]
    for copy in copies:
        copy.start()
    copies[0].wait()
    copies[1].wait()
    row = lax.broadcasted_iota(jnp.int32, (16, HD), 0)
    note = jnp.where(row == 0, lens[0] + lens[1], jnp.where(row == 1, groups[0], groups[1]))
    mine[:, 2 * KVW :] = note.astype(F32).astype(BF16)
    copies[2].wait()
    copies[3].wait()


def note_rows(refs, line):
    out = []
    for ref in refs:
        for part in range(4):
            block = ref[16 * part : 16 * part + 16, 2 * KVW :].astype(F32)
            out.append(block[line : line + 1])
    return out


def tie_kernel(*refs):
    pass


def plane_kernel(c0, c1, c2, c3, after, plane):
    for m, ref in enumerate((c0, c1, c2, c3)):
        plane[16 * m : 16 * m + 16, :] = ref[...]


def count_kernel(o0, o1, o2, o3, t0, t1, t2, t3, count):
    total = sum(note_rows((o0, o1, o2, o3, t0, t1, t2, t3), 0))
    count[...] = jnp.broadcast_to(total, count.shape)


def own_kernel(slot, comp_len, query, grad, kown, vown, after, q, do, lifted, pgrad, stats, lens, kbuf, vbuf, sems):
    rows = pl.ds(slot * CLEN, CLEN)
    small = [
        pltpu.make_async_copy(kown.at[rows], kbuf, sems.at[0]),
        pltpu.make_async_copy(vown.at[rows], vbuf, sems.at[1]),
        pltpu.make_async_copy(comp_len, lens, sems.at[10]),
    ]
    for copy in small:
        copy.start()
    copies = []
    for kv in range(KVH):
        cols = pl.ds(kv * QW, QW)
        copies.append(
            [
                pltpu.make_async_copy(query.at[rows, cols], q.at[:, cols], sems.at[2 + 2 * kv]),
                pltpu.make_async_copy(grad.at[rows, cols], do.at[:, cols], sems.at[3 + 2 * kv]),
            ]
        )
        for copy in copies[-1]:
            copy.start()
    row = lax.broadcasted_iota(jnp.int32, (CLEN, CLEN), 0)
    lane = lax.broadcasted_iota(jnp.int32, (CLEN, CLEN), 1)
    bias = jnp.where(row <= lane, 0.0, MASKED)
    bias = jnp.concatenate([bias, bias], 1)
    for copy in small:
        copy.wait()
    mask = jnp.where(row < lens[slot], 1.0, 0.0).astype(BF16)
    for kv in range(KVH):
        for copy in copies[kv]:
            copy.wait()
        keys = kbuf[:, cols_of(kv)]
        values = vbuf[:, cols_of(kv)]
        for pair in range(REP // 2):
            at = slice(pair * 256, pair * 256 + 256)
            dos = []
            for cols in heads_of(kv, pair):
                live = do[:, cols] * mask
                do[:, cols] = live
                dos.append(live)
            qs = jnp.concatenate([q[:, cols] for cols in heads_of(kv, pair)], 0)
            scores = dot_nt(keys, qs) * EXP2_SCALE + bias
            top = jnp.max(scores, axis=0, keepdims=True)
            part = jnp.exp2(scores - top)
            lifted[kv, :, at] = part
            stats[kv : kv + 1, at] = top
            stats[4 + kv : 5 + kv, at] = jnp.sum(part, axis=0, keepdims=True)
            pgrad[kv, :, at] = dot_nt(values, jnp.concatenate(dos, 0))


def prompt_kernel(
    slot, group, prompt_len, q, do, lifted, pgrad, stats, o0, o1, o2, o3, t0, t1, t2, t3, after, *refs
):
    before, refs = refs[: 2 * slot], refs[2 * slot :]
    ds, rowstats, kall, keep, send, vall, bias = refs
    y, z, c = position()
    near, far = (o0, o1, o2, o3), (t0, t1, t2, t3)
    row = lax.broadcasted_iota(jnp.int32, (PLEN, CLEN), 0)
    chunk = (((row // 16) % 4) ^ z) * 2 + ((row // 64) ^ c)
    place = chunk * 16 + row % 16
    for m in range(GPR):
        @pl.when((group[slot] ^ y) == m)
        def _():
            kall[0:64, :] = near[m][:, :KVW]
            kall[64:128, :] = far[m][:, :KVW]
            vall[0:64, :] = near[m][:, KVW : 2 * KVW]
            vall[64:128, :] = far[m][:, KVW : 2 * KVW]
    half = jnp.where(place < prompt_len[group[slot]], 0.0, MASKED)
    bias[...] = jnp.concatenate([half, half], 1)
    odd = group[slot] & 1
    if slot == 0:
        keep[1 - odd] = jnp.zeros((64, 2 * KVW), F32)
        send[1 - odd] = jnp.zeros((64, 2 * KVW), F32)
    else:
        keep[1 - odd] = before[0][1 - odd]
        send[1 - odd] = before[1][1 - odd]
    for kv in range(KVH):
        cols, vcols = cols_of(kv), cols_of(kv, KVW)
        keys, values = kall[:, cols], vall[:, cols]
        dv, dk = [], []
        for pair in range(REP // 2):
            at = slice(pair * 256, pair * 256 + 256)
            qs = jnp.concatenate([q[:, hc] for hc in heads_of(kv, pair)], 0)
            dos = jnp.concatenate([do[:, hc] for hc in heads_of(kv, pair)], 0)
            scores = dot_nt(keys, qs) * EXP2_SCALE + bias[...]
            top_own = stats[kv : kv + 1, at]
            top = jnp.maximum(jnp.max(scores, axis=0, keepdims=True), top_own)
            part = jnp.exp2(scores - top)
            shift = jnp.exp2(top_own - top)
            total = jnp.sum(part, axis=0, keepdims=True) + stats[4 + kv : 5 + kv, at] * shift
            inverse = 1.0 / total
            probs = part * inverse
            weights = probs.astype(BF16)
            factor = shift * inverse
            weights_own = (lifted[kv, :, at] * factor).astype(BF16)
            grad = dot_nt(values, dos)
            delta = jnp.sum(
                weights.astype(F32) * grad + weights_own.astype(F32) * pgrad[kv, :, at],
                axis=0, keepdims=True,
            )
            score = (probs * (grad - delta)).astype(BF16)
            ds[kv, :, at] = score
            rowstats[kv : kv + 1, at] = factor
            rowstats[4 + kv : 5 + kv, at] = delta
            dv.append((weights, dos))
            dk.append((score, qs))
        dv, dk = joined_dot(dv), joined_dot(dk)
        for out, old, part in ((keep, 0, slice(0, 64)), (send, 1, slice(64, 128))):
            for where, term in ((cols, dk[part]), (vcols, dv[part])):
                if slot:
                    term = term + before[old][odd, :, where]
                out[odd, :, where] = term


def grad_kernel(
    q0, do0, e0, g0, q1, do1, e1, g1, kown, ds0, row0, kall0, ds1, row1, kall1, after, dq, own
):
    slots = ((q0, do0, e0, g0, ds0, row0, kall0), (q1, do1, e1, g1, ds1, row1, kall1))
    for slot, (q, do, lifted, pgrad, ds, rowstats, kall) in enumerate(slots):
        rows = slice(slot * CLEN, (slot + 1) * CLEN)
        for kv in range(KVH):
            cols, vcols = cols_of(kv), cols_of(kv, KVW)
            keys = jnp.concatenate([kall[:, cols], kown[rows, cols]], 0)
            dv, dk = [], []
            for pair in range(REP // 2):
                at = slice(pair * 256, pair * 256 + 256)
                heads = heads_of(kv, pair)
                qs = jnp.concatenate([q[:, hc] for hc in heads], 0)
                dos = jnp.concatenate([do[:, hc] for hc in heads], 0)
                probs = lifted[kv, :, at] * rowstats[kv : kv + 1, at]
                delta = rowstats[4 + kv : 5 + kv, at]
                score = (probs * (pgrad[kv, :, at] - delta)).astype(BF16)
                dv.append((probs.astype(BF16), dos))
                dk.append((score, qs))
                scores = jnp.concatenate([ds[kv, :, at], score], 0)
                for j, hc in enumerate(heads):
                    dq[rows, hc] = dot_tn(scores[:, j * HD : (j + 1) * HD], keys)
            own[rows, cols] = joined_dot(dk)
            own[rows, vcols] = joined_dot(dv)


def scale_kernel(total, dq, own, after, query_grad, comp_key_grad, comp_value_grad, buf, kbuf, vbuf, sems):
    weight = ROWS / total[0:1, 0:1]
    scaled = weight * SCALE
    copies = []
    for i in range(KVH):
        cols = slice(i * QW, (i + 1) * QW)
        buf[:, cols] = (dq[:, cols] * scaled).astype(BF16)
        at = pl.ds(i * QW, QW)
        copies.append(pltpu.make_async_copy(buf.at[:, at], query_grad.at[:, at], sems.at[i]))
        copies[-1].start()
    kbuf[...] = (own[:, :KVW] * scaled).astype(BF16)
    vbuf[...] = (own[:, KVW:] * weight).astype(BF16)
    copies.append(pltpu.make_async_copy(kbuf, comp_key_grad, sems.at[4]))
    copies.append(pltpu.make_async_copy(vbuf, comp_value_grad, sems.at[5]))
    copies[-2].start()
    copies[-1].start()
    for copy in copies:
        copy.wait()


def chip_kernel(keep, got, k0, s1, s2, s3):
    for parity in range(2):
        both = keep[parity] + got[parity]
        k0[parity] = both[0:16]
        for m, out in enumerate((s1, s2, s3)):
            out[parity] = both[16 * (m + 1) : 16 * (m + 2)].astype(BF16)


def sum_kernel(near, far, k0, r1, r2, r3, after, also, k1, s1, s2, s3):
    y, _, _ = position()
    members = note_rows((near, far), 1) + note_rows((near, far), 2)
    for m, out in enumerate((k1, s1, s2, s3)):
        plane = y ^ m
        used = members[0] == plane.astype(F32)
        for member in members[1:]:
            used = used | (member == plane.astype(F32))
        used = jnp.broadcast_to(jnp.where(used, 1.0, 0.0), (16, HD))
        used = jnp.concatenate([used] * (2 * KVW // HD), 1)
        parity = plane & 1
        both = k0[parity]
        for ref in (r1, r2, r3):
            both += ref[parity].astype(F32)
        out[...] = (both * used).astype(out.dtype)


def last_kernel(total, k1, r1, r2, r3, dpk, dpv):
    weight = ROWS / total[0:1, 0:1]
    both = k1[...] + r1[...].astype(F32) + r2[...].astype(F32) + r3[...].astype(F32)
    dpk[...] = (both[:, :KVW] * (weight * SCALE)).astype(BF16)
    dpv[...] = (both[:, KVW:] * weight).astype(BF16)


SPECS = {
    "s": pl.BlockSpec(memory_space=pltpu.SMEM),
    "v": pl.BlockSpec(memory_space=VMEM),
    "a": pl.BlockSpec(memory_space=pl.ANY),
    "h": pl.BlockSpec(memory_space=pltpu.HBM),
}


def call(kernel, places, args, outs, out_places=None, scratch=(), limit=8):
    args = [
        pltpu.with_memory_space_constraint(x, pltpu.HBM) if p == "h" else x
        for p, x in zip(places, args, strict=True)
    ]
    return pl.pallas_call(
        kernel,
        out_shape=[jax.ShapeDtypeStruct(s, d) for s, d in outs],
        in_specs=[SPECS[p] for p in places],
        out_specs=[SPECS[p] for p in out_places or "v" * len(outs)],
        scratch_shapes=scratch,
        compiler_params=pltpu.CompilerParams(vmem_limit_bytes=limit * 2**20),
        cost_estimate=pl.CostEstimate(flops=1, bytes_accessed=1, transcendentals=0),
    )(*args)


def tie(x, after):
    return pl.pallas_call(
        tie_kernel,
        out_shape=jax.ShapeDtypeStruct(x.shape, x.dtype),
        in_specs=[SPECS["v"]] + [SPECS["a"]] * len(after),
        out_specs=SPECS["v"],
        input_output_aliases={0: 0},
        compiler_params=pltpu.CompilerParams(vmem_limit_bytes=2**20),
        cost_estimate=pl.CostEstimate(flops=1, bytes_accessed=1, transcendentals=0),
    )(x, *after)


def own_part(slot, comp_len, query, grad, kown, vown, after):
    def kernel(*refs):
        own_kernel(slot, *refs)

    return call(
        kernel, "hhhhha", [comp_len, query, grad, kown, vown, after],
        [
            ((CLEN, KVH * QW), BF16), ((CLEN, KVH * QW), BF16),
            ((KVH, CLEN, QW), F32), ((KVH, CLEN, QW), F32), ((8, QW), F32),
        ],
        scratch=[
            pltpu.SMEM((COMP,), jnp.int32), VMEM((CLEN, KVW), BF16), VMEM((CLEN, KVW), BF16),
            pltpu.SemaphoreType.DMA((11,)),
        ],
        limit=4
    )


def prompt_part(slot, group, prompt_len, parts, near, far, after, before=()):
    def kernel(*refs):
        prompt_kernel(slot, *refs)

    return call(
        kernel, "ss" + "v" * 13 + "a" + "v" * len(before),
        [group, prompt_len, *parts, *near, *far, after, *before],
        [
            ((KVH, PLEN, QW), BF16), ((8, QW), F32), ((PLEN, KVW), BF16),
            ((2, 64, 2 * KVW), F32), ((2, 64, 2 * KVW), F32),
        ],
        scratch=[VMEM((PLEN, KVW), BF16), VMEM((PLEN, 2 * CLEN), F32)],
        limit=4,
    )


def grad_part(parts0, parts1, kown, scores0, scores1, after):
    return call(
        grad_kernel, "v" * 15 + "a",
        [*parts0[:4], *parts1[:4], kown, *scores0, *scores1, after],
        [((COMP * CLEN, KVH * QW), F32), ((COMP * CLEN, 2 * KVW), F32)],
        limit=4,
    )


def scale_part(total, dq, own, after):
    rows = COMP * CLEN
    return call(
        scale_kernel, "vvva", [total, dq, own, after],
        [((rows, KVH * QW), BF16), ((rows, KVW), BF16), ((rows, KVW), BF16)], "hhh",
        scratch=[
            VMEM((rows, KVH * QW), BF16), VMEM((rows, KVW), BF16), VMEM((rows, KVW), BF16),
            pltpu.SemaphoreType.DMA((6,)),
        ],
        limit=8
    )


def swap(x, mask, axis="seq"):
    return lax.ppermute(x, axis, [(i, i ^ mask) for i in range(lax.axis_size(axis))])


def on_device(
    query, comp_key, comp_value, out_grad, prompt_key, prompt_value,
    prompt_len, comp_len, comp_group,
):
    wide = 2 * KVW
    (mine,) = call(
        pack_kernel, "hhhh", [comp_len, comp_group, prompt_key, prompt_value],
        [((16, wide + HD), BF16)],
        scratch=[
            pltpu.SMEM((COMP,), jnp.int32), pltpu.SMEM((COMP,), jnp.int32),
            pltpu.SemaphoreType.DMA((4,)),
        ],
    )
    chunks = [mine] + [swap(mine, 2 * m) for m in (1, 2, 3)]
    parts0 = own_part(0, comp_len, query, out_grad, comp_key, comp_value, mine)
    (plane,) = call(plane_kernel, "vvvva", [*chunks, parts0[4]], [((64, wide + HD), BF16)])
    near = [plane] + [swap(plane, 8 * m) for m in (1, 2, 3)]
    parts1 = own_part(1, comp_len, query, out_grad, comp_key, comp_value, plane)
    near[1] = tie(near[1], [parts1[4]])
    far = [swap(x, 1) for x in near]
    (count,) = call(count_kernel, "v" * 8, [*near, *far], [((8, HD), F32)])

    count1 = swap(count, 1, "grp")
    *scores0, keep, send = prompt_part(
        0, comp_group, prompt_len, parts0, near, far, count
    )
    count = count + count1
    *scores1, keep, send = prompt_part(
        1, comp_group, prompt_len, parts1, near, far, count, [keep, send]
    )
    got = swap(send, 1)
    k0, s1, s2, s3 = call(
        chip_kernel, "vv", [keep, got],
        [((2, 16, wide), F32)] + [((2, 16, wide), BF16)] * 3,
    )
    got = [swap(s, 2 * (m + 1)) for m, s in enumerate((s1, s2, s3))]
    dq, own = grad_part(parts0, parts1, comp_key, scores0, scores1, k0)
    count = count + swap(tie(count, [k0]), 2, "grp")
    k1, s1, s2, s3 = call(
        sum_kernel, "vvvvvvaa", [near[0], far[0], k0, *got, own, count],
        [((16, wide), F32)] + [((16, wide), BF16)] * 3,
    )
    got = [swap(s, 8 * (m + 1)) for m, s in enumerate((s1, s2, s3))]
    count = count + swap(tie(count, [k1]), 4, "grp")
    query_grad, comp_key_grad, comp_value_grad = scale_part(count, dq, own, k1)
    prompt_key_grad, prompt_value_grad = call(
        last_kernel, "vvvvv", [count, k1, *got], [((16, KVW), BF16)] * 2
    )
    return query_grad, comp_key_grad, comp_value_grad, prompt_key_grad, prompt_value_grad


def solution(mesh):
    rows, both = P(("grp", "seq"), None), P(("grp", "seq"))
    return jax.shard_map(
        on_device,
        mesh=mesh,
        in_specs=(rows,) * 6 + (P("grp"), both, both),
        out_specs=(rows,) * 5,
        check_vma=False,
    )
```

time: 456 us -> 59.4 us (0.13)
  waiting for transfers between devices: 200 us -> 14.2 us
  blocking collectives: 162 us -> 0 us
  local copies, waits for them, and re-layouts: 35.8 us -> 0.02 us
  starting transfers between devices: 0.08 us -> 26.4 us
  matrix products: 20.3 us -> 0 us
  other arithmetic: 20 us -> 0.01 us
  Pallas kernels: 0 us -> 17.7 us
  between operations: 16.2 us -> 0.86 us
    reduce_scatter x2 -> x0, waiting for transfers between devices: 200 us -> none  [the longest x1 143 us: on_device(): lax.psum_scatter(buffer_key, 'seq', scatter_dimension=0, tiled=True)]
    all_gather x2 -> x0, blocking collectives: 87.2 us -> none  [the longest x1 47 us: on_device(): lax.all_gather(prompt_key, 'seq', axis=0, tiled=True)]
    psum x1 -> x0, blocking collectives: 74.8 us -> none  [on_device(): live_total = lax.psum(jnp.sum(comp_len.astype(jnp.float32)), ('grp', 'seq'))]
    ppermute x0 -> x20, starting transfers between devices: none -> 26.4 us  [swap(): lax.ppermute(x, axis, [(i, i ^ mask) for i in range(lax.axis_size(axis))])]
    dynamic_slice x18 -> x0, local copies, waits for them, and re-layouts: 18.2 us -> none  [on_device(): lax.map(one_slot, (q_slots, grad_slots, key_slots, value_slots, near_lens))]
    pallas_call x0 -> x15, Pallas kernels: none -> 17.7 us  [the longest x12 17.6 us: call(): pl.pallas_call(kernel, out_shape=[jax.ShapeDtypeStruct(s, d) for s, d in...]
    ppermute x0 -> x20, waiting for transfers between devices: none -> 14.2 us  [swap(): lax.ppermute(x, axis, [(i, i ^ mask) for i in range(lax.axis_size(axis))])]
    dot_general x10 -> x0, matrix products: 13.5 us -> none  [the longest x2 6.26 us: slot_grads(): jnp.einsum('cgrd,lgd->grcl', grad_heads, value_heads, preferred_element_t...]
  transfers between devices with their start and end apart: 2 -> 20, of which waited for: 2 -> 7; matrix products, arithmetic and copies ran while one was open for 2% -> 0% of each run, Pallas kernels for 0% -> 22%
where the time goes in v1:
time: 59.4 us; the launch traced here: 59.2 us
  starting transfers between devices  26.4 us (44%)
  Pallas kernels  17.7 us (30%)
  waiting for transfers between devices  14.2 us (24%)
  between operations  0.86 us (1%)
    ppermute x20, starting transfers between devices, swap(): lax.ppermute(x, axis, [(i, i ^ mask) for i in range(lax.axis_size(axis))])  26.4 us
    pallas_call x12, Pallas kernels, call(): pl.pallas_call(kernel, out_shape=[jax.ShapeDtypeStruct(s, d) for s, d in...  17.6 us
    ppermute x20, waiting for transfers between devices, swap(): lax.ppermute(x, axis, [(i, i ^ mask) for i in range(lax.axis_size(axis))])  14.2 us
  transfers between devices with their start and end apart: 20, of which 7 were waited for; matrix products, arithmetic and copies ran while one was open for 0% of the time, Pallas kernels for 22%

profile of v1, /device:TPU:4, one launch (start us, length us, event | category | flops | bytes accessed | tf_op | source)
XLA Modules:
  0.0 59.2 jit_solution(13701770396067333148)
XLA Ops:
  0.6 0.8 %shard_map.128.refs_5_.c0 = bf16[16,1152]{1,0:T(8,128)(2,1)S(1)} custom-call(s32[2]{0:T(128)} %refs_0_.5, s32[2]{0:T(128)} %refs_0_.7, bf16[16,512]{1,0:T(8,128)(2,1)} %prompt_key.1, bf16[16,512]{1,0:T(8,128)(2,1)} %prompt_value.1), custom_call_target="tpu_custom_call" | custom-call | flops 1 | bytes 1 | tf_op jit(solution)/shard_map/pallas_call | solution.py:305
  1.4 2.0 %collective-permute-start = (bf16[16,1152]{1,0:T(8,128)(2,1)S(1)}, bf16[16,1152]{1,0:T(8,128)(2,1)S(1)}, u32[]{:S(2)}, u32[]{:S(2)}) collective-permute-start(bf16[16,1152]{1,0:T(8,128)(2,1)S(1)} %shard_map.128.refs_5_.c0), channel_id=1, source_target_pairs={{0,2},{1,3},{2,0},{3,1},{4,6},{5,7},{6,4},{7,5},{8,10},{9,11},{10,... | collective-permute-start | bytes 110600 | tf_op jit(solution)/shard_map/ppermute | solution.py:385
  3.4 3.3 %collective-permute-start.1 = (bf16[16,1152]{1,0:T(8,128)(2,1)S(1)}, bf16[16,1152]{1,0:T(8,128)(2,1)S(1)}, u32[]{:S(2)}, u32[]{:S(2)}) collective-permute-start(bf16[16,1152]{1,0:T(8,128)(2,1)S(1)} %shard_map.128.refs_5_.c0), channel_id=1, source_target_pairs={{0,4},{1,5},{2,6},{3,7},{4,0},{5,1},{6,2},{7,3},{8,12},{9,13},{10,... | collective-permute-start | bytes 110600 | tf_op jit(solution)/shard_map/ppermute | solution.py:385
  6.7 0.0 collective-permute-start.2
  6.7 2.7 %shard_map.129 = (bf16[128,4096]{1,0:T(8,128)(2,1)S(1)}, bf16[128,4096]{1,0:T(8,128)(2,1)S(1)}, f32[4,128,1024]{2,1,0:T(8,128)S(1)}, f32[4,128,1024]{2,1,0:T(8,128)S(1)}, f32[8,1024]{1,0:T(8,128)S(1)}) custom-call(s32[2]{0:T(128)} %refs_0_.5, bf16[256,4096]{1,0:T(8,128)(2,1)} %refs_1_.5, bf16[256,4096]{1,0:T(8,128)(2,1)} %refs_2_.3, bf16[256,512]{1,0:T(8,128)(2,1)} %kown.1, ...), custom_call_target="tpu_custom_call" | custom-call | flops 1 | bytes 1 | tf_op jit(solution)/shard_map/pallas_call | solution.py:305
  9.4 0.0 collective-permute-done.c1
  9.4 0.0 collective-permute-done.1.c2
  9.5 3.0 %collective-permute-done.2.c3 = bf16[16,1152]{1,0:T(8,128)(2,1)S(1)} collective-permute-done((bf16[16,1152]{1,0:T(8,128)(2,1)S(1)}, bf16[16,1152]{1,0:T(8,128)(2,1)S(1)}, u32[]{:S(2)}, u32[]{:S(2)}) %collective-permute-start.2) | collective-permute-done | bytes 36896 | tf_op jit(solution)/shard_map/ppermute | solution.py:385
  12.5 0.0 copy-start.1
  12.5 0.0 copy-start.2
  12.5 1.7 %collective-permute-start.3 = (bf16[64,1152]{1,0:T(8,128)(2,1)S(1)}, bf16[64,1152]{1,0:T(8,128)(2,1)S(1)}, u32[]{:S(2)}, u32[]{:S(2)}) collective-permute-start(bf16[64,1152]{1,0:T(8,128)(2,1)S(1)} %shard_map.130.refs_5_.o0.refs_7_.near), channel_id=1, source_target_pairs={{0,8},{1,9},{2,10},{3,11},{4,12},{5,13},{6,14},{7,15},{8,0},{9,1},... | collective-permute-start | bytes 442376 | tf_op jit(solution)/shard_map/ppermute | solution.py:385
  14.2 2.9 %collective-permute-start.4 = (bf16[64,1152]{1,0:T(8,128)(2,1)S(1)}, bf16[64,1152]{1,0:T(8,128)(2,1)S(1)}, u32[]{:S(2)}, u32[]{:S(2)}) collective-permute-start(bf16[64,1152]{1,0:T(8,128)(2,1)S(1)} %shard_map.130.refs_5_.o0.refs_7_.near), channel_id=1, source_target_pairs={{0,16},{1,17},{2,18},{3,19},{4,20},{5,21},{6,22},{7,23},{8,24},{9,... | collective-permute-start | bytes 442376 | tf_op jit(solution)/shard_map/ppermute | solution.py:385
  17.1 0.2 collective-permute-start.5
  17.3 2.7 %shard_map.131 = (bf16[128,4096]{1,0:T(8,128)(2,1)S(1)}, bf16[128,4096]{1,0:T(8,128)(2,1)S(1)}, f32[4,128,1024]{2,1,0:T(8,128)S(1)}, f32[4,128,1024]{2,1,0:T(8,128)S(1)}, f32[8,1024]{1,0:T(8,128)S(1)}) custom-call(s32[2]{0:T(128)} %refs_0_.5, bf16[256,4096]{1,0:T(8,128)(2,1)} %refs_1_.5, bf16[256,4096]{1,0:T(8,128)(2,1)} %refs_2_.3, bf16[256,512]{1,0:T(8,128)(2,1)} %kown.1, ...), custom_call_target="tpu_custom_call" | custom-call | flops 1 | bytes 1 | tf_op jit(solution)/shard_map/pallas_call | solution.py:305
  20.0 0.1 collective-permute-start.6
  20.1 0.0 collective-permute-done.3.refs_0_
  20.1 0.5 collective-permute-start.7
  20.6 1.5 %collective-permute-done.4.o2.refs_9_ = bf16[64,1152]{1,0:T(8,128)(2,1)S(1)} collective-permute-done((bf16[64,1152]{1,0:T(8,128)(2,1)S(1)}, bf16[64,1152]{1,0:T(8,128)(2,1)S(1)}, u32[]{:S(2)}, u32[]{:S(2)}) %collective-permute-start.4) | collective-permute-done | bytes 147488 | tf_op jit(solution)/shard_map/ppermute | solution.py:385
  22.1 0.0 collective-permute-start.8
  22.1 1.6 %collective-permute-done.5.o3.refs_10_ = bf16[64,1152]{1,0:T(8,128)(2,1)S(1)} collective-permute-done((bf16[64,1152]{1,0:T(8,128)(2,1)S(1)}, bf16[64,1152]{1,0:T(8,128)(2,1)S(1)}, u32[]{:S(2)}, u32[]{:S(2)}) %collective-permute-start.5) | collective-permute-done | bytes 147488 | tf_op jit(solution)/shard_map/ppermute | solution.py:385
  23.6 0.0 collective-permute-start.9
  23.6 0.0 collective-permute-done.6.t0.refs_11_.far
  23.6 0.0 collective-permute-done.7.t1.refs_12_
  23.7 0.0 collective-permute-done.8.t2.refs_13_
  23.7 1.3 %collective-permute-done.9.t3.refs_14_ = bf16[64,1152]{1,0:T(8,128)(2,1)S(1)} collective-permute-done((bf16[64,1152]{1,0:T(8,128)(2,1)S(1)}, bf16[64,1152]{1,0:T(8,128)(2,1)S(1)}, u32[]{:S(2)}, u32[]{:S(2)}) %collective-permute-start.9) | collective-permute-done | bytes 147488 | tf_op jit(solution)/shard_map/ppermute | solution.py:385
  25.1 4.8 %collective-permute-start.10 = (f32[8,128]{1,0:T(8,128)S(1)}, f32[8,128]{1,0:T(8,128)S(1)}, u32[]{:S(2)}, u32[]{:S(2)}) collective-permute-start(f32[8,128]{1,0:T(8,128)S(1)} %shard_map.133.refs_15_), channel_id=1, source_target_pairs={{0,32},{32,0},{64,96},{96,64},{128,160},{160,128},{192,224},{224,1... | collective-permute-start | bytes 12296 | tf_op jit(solution)/shard_map/ppermute | solution.py:385
  29.8 0.0 copy-done.1
  29.8 0.0 copy-done.2
  29.8 3.0 %shard_map.134 = (bf16[4,128,1024]{2,1,0:T(8,128)(2,1)S(1)}, f32[8,1024]{1,0:T(8,128)S(1)}, bf16[128,512]{1,0:T(8,128)(2,1)S(1)}, f32[2,64,1024]{2,1,0:T(8,128)S(1)}, f32[2,64,1024]{2,1,0:T(8,128)S(1)}) custom-call(s32[2]{0:T(128)S(1)} %copy-done.1, s32[4]{0:T(128)S(1)} %copy-done.2, bf16[128,4096]{1,0:T(8,128)(2,1)S(1)} %get-tuple-element.46.refs_2_.q0, ...), custom_call_target="tpu_custom_call" | custom-call | flops 1 | bytes 1 | tf_op jit(solution)/shard_map/pallas_call | solution.py:305
  32.8 0.0 collective-permute-done.10
  32.8 0.0 copy-start
  32.8 3.1 %shard_map.135 = (bf16[4,128,1024]{2,1,0:T(8,128)(2,1)S(1)}, f32[8,1024]{1,0:T(8,128)S(1)}, bf16[128,512]{1,0:T(8,128)(2,1)S(1)}, f32[2,64,1024]{2,1,0:T(8,128)S(1)}, f32[2,64,1024]{2,1,0:T(8,128)S(1)}) custom-call(s32[2]{0:T(128)S(1)} %copy-done.1, s32[4]{0:T(128)S(1)} %copy-done.2, bf16[128,4096]{1,0:T(8,128)(2,1)S(1)} %get-tuple-element.42.refs_2_.q1, ...), custom_call_target="tpu_custom_call" | custom-call | flops 1 | bytes 1 | tf_op jit(solution)/shard_map/pallas_call | solution.py:305
  36.0 0.1 collective-permute-start.11
  36.1 1.9 %collective-permute-done.11.got = f32[2,64,1024]{2,1,0:T(8,128)S(1)} collective-permute-done((f32[2,64,1024]{2,1,0:T(8,128)S(1)}, f32[2,64,1024]{2,1,0:T(8,128)S(1)}, u32[]{:S(2)}, u32[]{:S(2)}) %collective-permute-start.11) | collective-permute-done | bytes 524320 | tf_op jit(solution)/shard_map/ppermute | solution.py:385
  38.0 0.1 shard_map.136
  38.0 0.1 collective-permute-start.13
  38.1 2.5 %collective-permute-start.14 = (bf16[2,16,1024]{2,1,0:T(8,128)(2,1)S(1)}, bf16[2,16,1024]{2,1,0:T(8,128)(2,1)S(1)}, u32[]{:S(2)}, u32[]{:S(2)}) collective-permute-start(bf16[2,16,1024]{2,1,0:T(8,128)(2,1)S(1)} %get-tuple-element.56), channel_id=1, source_target_pairs={{0,4},{1,5},{2,6},{3,7},{4,0},{5,1},{6,2},{7,3},{8,12},{9,13},{10,... | collective-permute-start | bytes 196616 | tf_op jit(solution)/shard_map/ppermute | solution.py:385
  40.6 1.9 %collective-permute-start.15 = (bf16[2,16,1024]{2,1,0:T(8,128)(2,1)S(1)}, bf16[2,16,1024]{2,1,0:T(8,128)(2,1)S(1)}, u32[]{:S(2)}, u32[]{:S(2)}) collective-permute-start(bf16[2,16,1024]{2,1,0:T(8,128)(2,1)S(1)} %get-tuple-element.57), channel_id=1, source_target_pairs={{0,6},{1,7},{2,4},{3,5},{4,2},{5,3},{6,0},{7,1},{8,14},{9,15},{10,... | collective-permute-start | bytes 196616 | tf_op jit(solution)/shard_map/ppermute | solution.py:385
  42.5 1.2 %collective-permute-start.12 = (f32[8,128]{1,0:T(8,128)S(1)}, f32[8,128]{1,0:T(8,128)S(1)}, u32[]{:S(2)}, u32[]{:S(2)}) collective-permute-start(f32[8,128]{1,0:T(8,128)S(1)} %shard_map.137), channel_id=1, source_target_pairs={{0,64},{32,96},{64,0},{96,32},{128,192},{160,224},{192,128},{224,1... | collective-permute-start | bytes 12296 | tf_op jit(solution)/shard_map/ppermute | solution.py:385
  43.7 0.0 copy-done
  43.7 2.8 %shard_map.138 = (f32[256,4096]{1,0:T(8,128)S(1)}, f32[256,1024]{1,0:T(8,128)S(1)}) custom-call(bf16[128,4096]{1,0:T(8,128)(2,1)S(1)} %get-tuple-element.46.refs_2_.q0, bf16[128,4096]{1,0:T(8,128)(2,1)S(1)} %get-tuple-element.47.refs_3_.do0, f32[4,128,1024]{2,1,0:T(8,128)S(1)} %get-tuple-element.48.refs_4_.e0, ...), custom_call_target="tpu_custom_call" | custom-call | flops 1 | bytes 1 | tf_op jit(solution)/shard_map/pallas_call | solution.py:305
  46.4 0.0 collective-permute-done.12
  46.5 0.0 collective-permute-done.13.r1
  46.5 0.3 collective-permute-done.14.r2
  46.8 0.0 collective-permute-done.15.r3
  46.8 0.1 shard_map.139
  46.9 0.1 collective-permute-start.17
  47.0 2.4 %collective-permute-start.18 = (bf16[16,1024]{1,0:T(8,128)(2,1)S(1)}, bf16[16,1024]{1,0:T(8,128)(2,1)S(1)}, u32[]{:S(2)}, u32[]{:S(2)}) collective-permute-start(bf16[16,1024]{1,0:T(8,128)(2,1)S(1)} %get-tuple-element.71), channel_id=1, source_target_pairs={{0,16},{1,17},{2,18},{3,19},{4,20},{5,21},{6,22},{7,23},{8,24},{9,... | collective-permute-start | bytes 98312 | tf_op jit(solution)/shard_map/ppermute | solution.py:385
  49.4 2.2 %collective-permute-start.19 = (bf16[16,1024]{1,0:T(8,128)(2,1)S(1)}, bf16[16,1024]{1,0:T(8,128)(2,1)S(1)}, u32[]{:S(2)}, u32[]{:S(2)}) collective-permute-start(bf16[16,1024]{1,0:T(8,128)(2,1)S(1)} %get-tuple-element.72), channel_id=1, source_target_pairs={{0,24},{1,25},{2,26},{3,27},{4,28},{5,29},{6,30},{7,31},{8,16},{9,... | collective-permute-start | bytes 98312 | tf_op jit(solution)/shard_map/ppermute | solution.py:385
  51.7 0.5 collective-permute-start.16
  52.2 4.6 %collective-permute-done.16 = f32[8,128]{1,0:T(8,128)S(1)} collective-permute-done((f32[8,128]{1,0:T(8,128)S(1)}, f32[8,128]{1,0:T(8,128)S(1)}, u32[]{:S(2)}, u32[]{:S(2)}) %collective-permute-start.16) | collective-permute-done | bytes 4128 | tf_op jit(solution)/shard_map/ppermute | solution.py:385
  56.8 1.7 %shard_map.141 = (bf16[256,4096]{1,0:T(8,128)(2,1)}, bf16[256,512]{1,0:T(8,128)(2,1)}, bf16[256,512]{1,0:T(8,128)(2,1)}) custom-call(f32[8,128]{1,0:T(8,128)S(1)} %add.11.total, f32[256,4096]{1,0:T(8,128)S(1)} %get-tuple-element.66.dq, f32[256,1024]{1,0:T(8,128)S(1)} %get-tuple-element.64.after.own, f32[16,1024]{1,0:T(8,128)S(1)} %get-tuple-element.65.refs_1_.after.k1), custom_call_target="tpu_custom_call" | custom-call | flops 1 | bytes 1 | tf_op jit(solution)/shard_map/pallas_call | solution.py:305
  58.5 0.0 collective-permute-done.17.r1
  58.5 0.0 collective-permute-done.18.r2
  58.5 0.0 collective-permute-done.19.r3
  58.5 0.7 %shard_map.142 = (bf16[16,512]{1,0:T(8,128)(2,1)}, bf16[16,512]{1,0:T(8,128)(2,1)}) custom-call(f32[8,128]{1,0:T(8,128)S(1)} %add.11.total, f32[16,1024]{1,0:T(8,128)S(1)} %get-tuple-element.65.refs_1_.after.k1, bf16[16,1024]{1,0:T(8,128)(2,1)S(1)} %collective-permute-done.17.r1, bf16[16,1024]{1,0:T(8,128)(2,1)S(1)} %collective-permute-done.18.r2, ...), custom_call_target="tpu_custom_call" | custom-call | flops 1 | bytes 1 | tf_op jit(solution)/shard_map/pallas_call | solution.py:305
  (10 shorter events, 0.1 us)
Async XLA Ops:
  1.4 8.0 %collective-permute-start = (bf16[16,1152]{1,0:T(8,128)(2,1)S(1)}, bf16[16,1152]{1,0:T(8,128)(2,1)S(1)}, u32[]{:S(2)}, u32[]{:S(2)}) collective-permute-start(bf16[16,1152]{1,0:T(8,128)(2,1)S(1)} %shard_map.128.refs_5_.c0), channel_id=1, source_target_pairs={{0,2},{1,3},{2,0},{3,1},{4,6},{5,7},{6,4},{7,5},{8,10},{9,11},{10,... | collective-permute-start | bytes 110600 | tf_op jit(solution)/shard_map/ppermute | solution.py:385
  3.4 6.0 %collective-permute-start.1 = (bf16[16,1152]{1,0:T(8,128)(2,1)S(1)}, bf16[16,1152]{1,0:T(8,128)(2,1)S(1)}, u32[]{:S(2)}, u32[]{:S(2)}) collective-permute-start(bf16[16,1152]{1,0:T(8,128)(2,1)S(1)} %shard_map.128.refs_5_.c0), channel_id=1, source_target_pairs={{0,4},{1,5},{2,6},{3,7},{4,0},{5,1},{6,2},{7,3},{8,12},{9,13},{10,... | collective-permute-start | bytes 110600 | tf_op jit(solution)/shard_map/ppermute | solution.py:385
  6.7 5.8 %collective-permute-start.2 = (bf16[16,1152]{1,0:T(8,128)(2,1)S(1)}, bf16[16,1152]{1,0:T(8,128)(2,1)S(1)}, u32[]{:S(2)}, u32[]{:S(2)}) collective-permute-start(bf16[16,1152]{1,0:T(8,128)(2,1)S(1)} %shard_map.128.refs_5_.c0), channel_id=1, source_target_pairs={{0,6},{1,7},{2,4},{3,5},{4,2},{5,3},{6,0},{7,1},{8,14},{9,15},{10,... | collective-permute-start | bytes 110600 | tf_op jit(solution)/shard_map/ppermute | solution.py:385
  12.5 17.4 %copy-start.1 = (s32[2]{0:T(128)S(1)}, s32[2]{0:T(128)}, u32[]{:S(2)}) copy-start(s32[2]{0:T(128)} %refs_0_.7) | copy-start | bytes 28
  12.5 17.3 %copy-start.2 = (s32[4]{0:T(128)S(1)}, s32[4]{0:T(128)}, u32[]{:S(2)}) copy-start(s32[4]{0:T(128)} %refs_1_.7) | copy-start | bytes 52
  12.5 7.6 %collective-permute-start.3 = (bf16[64,1152]{1,0:T(8,128)(2,1)S(1)}, bf16[64,1152]{1,0:T(8,128)(2,1)S(1)}, u32[]{:S(2)}, u32[]{:S(2)}) collective-permute-start(bf16[64,1152]{1,0:T(8,128)(2,1)S(1)} %shard_map.130.refs_5_.o0.refs_7_.near), channel_id=1, source_target_pairs={{0,8},{1,9},{2,10},{3,11},{4,12},{5,13},{6,14},{7,15},{8,0},{9,1},... | collective-permute-start | bytes 442376 | tf_op jit(solution)/shard_map/ppermute | solution.py:385
  14.2 7.9 %collective-permute-start.4 = (bf16[64,1152]{1,0:T(8,128)(2,1)S(1)}, bf16[64,1152]{1,0:T(8,128)(2,1)S(1)}, u32[]{:S(2)}, u32[]{:S(2)}) collective-permute-start(bf16[64,1152]{1,0:T(8,128)(2,1)S(1)} %shard_map.130.refs_5_.o0.refs_7_.near), channel_id=1, source_target_pairs={{0,16},{1,17},{2,18},{3,19},{4,20},{5,21},{6,22},{7,23},{8,24},{9,... | collective-permute-start | bytes 442376 | tf_op jit(solution)/shard_map/ppermute | solution.py:385
  17.1 6.6 %collective-permute-start.5 = (bf16[64,1152]{1,0:T(8,128)(2,1)S(1)}, bf16[64,1152]{1,0:T(8,128)(2,1)S(1)}, u32[]{:S(2)}, u32[]{:S(2)}) collective-permute-start(bf16[64,1152]{1,0:T(8,128)(2,1)S(1)} %shard_map.130.refs_5_.o0.refs_7_.near), channel_id=1, source_target_pairs={{0,24},{1,25},{2,26},{3,27},{4,28},{5,29},{6,30},{7,31},{8,16},{9,... | collective-permute-start | bytes 442376 | tf_op jit(solution)/shard_map/ppermute | solution.py:385
  20.0 3.6 %collective-permute-start.6 = (bf16[64,1152]{1,0:T(8,128)(2,1)S(1)}, bf16[64,1152]{1,0:T(8,128)(2,1)S(1)}, u32[]{:S(2)}, u32[]{:S(2)}) collective-permute-start(bf16[64,1152]{1,0:T(8,128)(2,1)S(1)} %shard_map.130.refs_5_.o0.refs_7_.near), channel_id=1, source_target_pairs={{0,1},{1,0},{2,3},{3,2},{4,5},{5,4},{6,7},{7,6},{8,9},{9,8},{10,11... | collective-permute-start | bytes 442376 | tf_op jit(solution)/shard_map/ppermute | solution.py:385
  20.1 3.5 %collective-permute-start.7 = (bf16[64,1152]{1,0:T(8,128)(2,1)S(1)}, bf16[64,1152]{1,0:T(8,128)(2,1)S(1)}, u32[]{:S(2)}, u32[]{:S(2)}) collective-permute-start(bf16[64,1152]{1,0:T(8,128)(2,1)S(1)} %shard_map.132.o1.refs_8_), channel_id=1, source_target_pairs={{0,1},{1,0},{2,3},{3,2},{4,5},{5,4},{6,7},{7,6},{8,9},{9,8},{10,11... | collective-permute-start | bytes 442376 | tf_op jit(solution)/shard_map/ppermute | solution.py:385
  22.1 1.6 %collective-permute-start.8 = (bf16[64,1152]{1,0:T(8,128)(2,1)S(1)}, bf16[64,1152]{1,0:T(8,128)(2,1)S(1)}, u32[]{:S(2)}, u32[]{:S(2)}) collective-permute-start(bf16[64,1152]{1,0:T(8,128)(2,1)S(1)} %collective-permute-done.4.o2.refs_9_), channel_id=1, source_target_pairs={{0,1},{1,0},{2,3},{3,2},{4,5},{5,4},{6,7},{7,6},{8,9},{9,8},{10,11... | collective-permute-start | bytes 442376 | tf_op jit(solution)/shard_map/ppermute | solution.py:385
  23.6 1.4 %collective-permute-start.9 = (bf16[64,1152]{1,0:T(8,128)(2,1)S(1)}, bf16[64,1152]{1,0:T(8,128)(2,1)S(1)}, u32[]{:S(2)}, u32[]{:S(2)}) collective-permute-start(bf16[64,1152]{1,0:T(8,128)(2,1)S(1)} %collective-permute-done.5.o3.refs_10_), channel_id=1, source_target_pairs={{0,1},{1,0},{2,3},{3,2},{4,5},{5,4},{6,7},{7,6},{8,9},{9,8},{10,11... | collective-permute-start | bytes 442376 | tf_op jit(solution)/shard_map/ppermute | solution.py:385
  25.1 7.8 %collective-permute-start.10 = (f32[8,128]{1,0:T(8,128)S(1)}, f32[8,128]{1,0:T(8,128)S(1)}, u32[]{:S(2)}, u32[]{:S(2)}) collective-permute-start(f32[8,128]{1,0:T(8,128)S(1)} %shard_map.133.refs_15_), channel_id=1, source_target_pairs={{0,32},{32,0},{64,96},{96,64},{128,160},{160,128},{192,224},{224,1... | collective-permute-start | bytes 12296 | tf_op jit(solution)/shard_map/ppermute | solution.py:385
  32.8 10.9 %copy-start = (bf16[256,512]{1,0:T(8,128)(2,1)S(1)}, bf16[256,512]{1,0:T(8,128)(2,1)}, u32[]{:S(2)}) copy-start(bf16[256,512]{1,0:T(8,128)(2,1)} %kown.1) | copy-start | bytes 786436
  36.0 2.0 %collective-permute-start.11 = (f32[2,64,1024]{2,1,0:T(8,128)S(1)}, f32[2,64,1024]{2,1,0:T(8,128)S(1)}, u32[]{:S(2)}, u32[]{:S(2)}) collective-permute-start(f32[2,64,1024]{2,1,0:T(8,128)S(1)} %get-tuple-element.53), channel_id=1, source_target_pairs={{0,1},{1,0},{2,3},{3,2},{4,5},{5,4},{6,7},{7,6},{8,9},{9,8},{10,11... | collective-permute-start | bytes 1572872 | tf_op jit(solution)/shard_map/ppermute | solution.py:385
  38.0 8.5 %collective-permute-start.13 = (bf16[2,16,1024]{2,1,0:T(8,128)(2,1)S(1)}, bf16[2,16,1024]{2,1,0:T(8,128)(2,1)S(1)}, u32[]{:S(2)}, u32[]{:S(2)}) collective-permute-start(bf16[2,16,1024]{2,1,0:T(8,128)(2,1)S(1)} %get-tuple-element.55), channel_id=1, source_target_pairs={{0,2},{1,3},{2,0},{3,1},{4,6},{5,7},{6,4},{7,5},{8,10},{9,11},{10,... | collective-permute-start | bytes 196616 | tf_op jit(solution)/shard_map/ppermute | solution.py:385
  38.1 8.7 %collective-permute-start.14 = (bf16[2,16,1024]{2,1,0:T(8,128)(2,1)S(1)}, bf16[2,16,1024]{2,1,0:T(8,128)(2,1)S(1)}, u32[]{:S(2)}, u32[]{:S(2)}) collective-permute-start(bf16[2,16,1024]{2,1,0:T(8,128)(2,1)S(1)} %get-tuple-element.56), channel_id=1, source_target_pairs={{0,4},{1,5},{2,6},{3,7},{4,0},{5,1},{6,2},{7,3},{8,12},{9,13},{10,... | collective-permute-start | bytes 196616 | tf_op jit(solution)/shard_map/ppermute | solution.py:385
  40.6 6.2 %collective-permute-start.15 = (bf16[2,16,1024]{2,1,0:T(8,128)(2,1)S(1)}, bf16[2,16,1024]{2,1,0:T(8,128)(2,1)S(1)}, u32[]{:S(2)}, u32[]{:S(2)}) collective-permute-start(bf16[2,16,1024]{2,1,0:T(8,128)(2,1)S(1)} %get-tuple-element.57), channel_id=1, source_target_pairs={{0,6},{1,7},{2,4},{3,5},{4,2},{5,3},{6,0},{7,1},{8,14},{9,15},{10,... | collective-permute-start | bytes 196616 | tf_op jit(solution)/shard_map/ppermute | solution.py:385
  42.5 4.0 %collective-permute-start.12 = (f32[8,128]{1,0:T(8,128)S(1)}, f32[8,128]{1,0:T(8,128)S(1)}, u32[]{:S(2)}, u32[]{:S(2)}) collective-permute-start(f32[8,128]{1,0:T(8,128)S(1)} %shard_map.137), channel_id=1, source_target_pairs={{0,64},{32,96},{64,0},{96,32},{128,192},{160,224},{192,128},{224,1... | collective-permute-start | bytes 12296 | tf_op jit(solution)/shard_map/ppermute | solution.py:385
  46.9 11.6 %collective-permute-start.17 = (bf16[16,1024]{1,0:T(8,128)(2,1)S(1)}, bf16[16,1024]{1,0:T(8,128)(2,1)S(1)}, u32[]{:S(2)}, u32[]{:S(2)}) collective-permute-start(bf16[16,1024]{1,0:T(8,128)(2,1)S(1)} %get-tuple-element.70), channel_id=1, source_target_pairs={{0,8},{1,9},{2,10},{3,11},{4,12},{5,13},{6,14},{7,15},{8,0},{9,1},... | collective-permute-start | bytes 98312 | tf_op jit(solution)/shard_map/ppermute | solution.py:385
  47.0 11.5 %collective-permute-start.18 = (bf16[16,1024]{1,0:T(8,128)(2,1)S(1)}, bf16[16,1024]{1,0:T(8,128)(2,1)S(1)}, u32[]{:S(2)}, u32[]{:S(2)}) collective-permute-start(bf16[16,1024]{1,0:T(8,128)(2,1)S(1)} %get-tuple-element.71), channel_id=1, source_target_pairs={{0,16},{1,17},{2,18},{3,19},{4,20},{5,21},{6,22},{7,23},{8,24},{9,... | collective-permute-start | bytes 98312 | tf_op jit(solution)/shard_map/ppermute | solution.py:385
  49.4 9.1 %collective-permute-start.19 = (bf16[16,1024]{1,0:T(8,128)(2,1)S(1)}, bf16[16,1024]{1,0:T(8,128)(2,1)S(1)}, u32[]{:S(2)}, u32[]{:S(2)}) collective-permute-start(bf16[16,1024]{1,0:T(8,128)(2,1)S(1)} %get-tuple-element.72), channel_id=1, source_target_pairs={{0,24},{1,25},{2,26},{3,27},{4,28},{5,29},{6,30},{7,31},{8,16},{9,... | collective-permute-start | bytes 98312 | tf_op jit(solution)/shard_map/ppermute | solution.py:385
  51.7 5.1 %collective-permute-start.16 = (f32[8,128]{1,0:T(8,128)S(1)}, f32[8,128]{1,0:T(8,128)S(1)}, u32[]{:S(2)}, u32[]{:S(2)}) collective-permute-start(f32[8,128]{1,0:T(8,128)S(1)} %shard_map.140), channel_id=1, source_target_pairs={{0,128},{32,160},{64,192},{96,224},{128,0},{160,32},{192,64},{224,... | collective-permute-start | bytes 12296 | tf_op jit(solution)/shard_map/ppermute | solution.py:385

commit v2 on v1

--- a/solution.py
+++ b/solution.py
@@ -147,12 +147,22 @@
 
 
 def prompt_kernel(
-    slot, group, prompt_len, q, do, lifted, pgrad, stats, o0, o1, o2, o3, t0, t1, t2, t3, after, *refs
+    group, prompt_len, q0, do0, e0, g0, st0, q1, do1, e1, g1, st1,
+    o0, o1, o2, o3, t0, t1, t2, t3, after,
+    ds0, row0, kall0, ds1, row1, kall1, keep, send, vall, bias,
 ):
-    before, refs = refs[: 2 * slot], refs[2 * slot :]
-    ds, rowstats, kall, keep, send, vall, bias = refs
+    keep[...] = jnp.zeros_like(keep)
+    send[...] = jnp.zeros_like(send)
+    near, far = (o0, o1, o2, o3), (t0, t1, t2, t3)
+    slots = ((q0, do0, e0, g0, st0, ds0, row0, kall0), (q1, do1, e1, g1, st1, ds1, row1, kall1))
+    for slot, refs in enumerate(slots):
+        prompt_slot(slot, group, prompt_len, near, far, *refs, keep, send, vall.at[slot], bias.at[slot])
+
+
+def prompt_slot(
+    slot, group, prompt_len, near, far, q, do, lifted, pgrad, stats, ds, rowstats, kall, keep, send, vall, bias
+):
     y, z, c = position()
-    near, far = (o0, o1, o2, o3), (t0, t1, t2, t3)
     row = lax.broadcasted_iota(jnp.int32, (PLEN, CLEN), 0)
     chunk = (((row // 16) % 4) ^ z) * 2 + ((row // 64) ^ c)
     place = chunk * 16 + row % 16
@@ -166,48 +176,44 @@
     half = jnp.where(place < prompt_len[group[slot]], 0.0, MASKED)
     bias[...] = jnp.concatenate([half, half], 1)
     odd = group[slot] & 1
-    if slot == 0:
-        keep[1 - odd] = jnp.zeros((64, 2 * KVW), F32)
-        send[1 - odd] = jnp.zeros((64, 2 * KVW), F32)
-    else:
-        keep[1 - odd] = before[0][1 - odd]
-        send[1 - odd] = before[1][1 - odd]
-    for kv in range(KVH):
-        cols, vcols = cols_of(kv), cols_of(kv, KVW)
-        keys, values = kall[:, cols], vall[:, cols]
-        dv, dk = [], []
+    for kvs in ((0, 1), (2, 3)):
+        terms = {kv: ([], []) for kv in kvs}
         for pair in range(REP // 2):
-            at = slice(pair * 256, pair * 256 + 256)
-            qs = jnp.concatenate([q[:, hc] for hc in heads_of(kv, pair)], 0)
-            dos = jnp.concatenate([do[:, hc] for hc in heads_of(kv, pair)], 0)
-            scores = dot_nt(keys, qs) * EXP2_SCALE + bias[...]
-            top_own = stats[kv : kv + 1, at]
-            top = jnp.maximum(jnp.max(scores, axis=0, keepdims=True), top_own)
-            part = jnp.exp2(scores - top)
-            shift = jnp.exp2(top_own - top)
-            total = jnp.sum(part, axis=0, keepdims=True) + stats[4 + kv : 5 + kv, at] * shift
-            inverse = 1.0 / total
-            probs = part * inverse
-            weights = probs.astype(BF16)
-            factor = shift * inverse
-            weights_own = (lifted[kv, :, at] * factor).astype(BF16)
-            grad = dot_nt(values, dos)
-            delta = jnp.sum(
-                weights.astype(F32) * grad + weights_own.astype(F32) * pgrad[kv, :, at],
-                axis=0, keepdims=True,
-            )
-            score = (probs * (grad - delta)).astype(BF16)
-            ds[kv, :, at] = score
-            rowstats[kv : kv + 1, at] = factor
-            rowstats[4 + kv : 5 + kv, at] = delta
-            dv.append((weights, dos))
-            dk.append((score, qs))
-        dv, dk = joined_dot(dv), joined_dot(dk)
-        for out, old, part in ((keep, 0, slice(0, 64)), (send, 1, slice(64, 128))):
-            for where, term in ((cols, dk[part]), (vcols, dv[part])):
-                if slot:
-                    term = term + before[old][odd, :, where]
-                out[odd, :, where] = term
+            for kv in kvs:
+                dv, dk = terms[kv]
+                cols = cols_of(kv)
+                keys, values = kall[:, cols], vall[:, cols]
+                at = slice(pair * 256, pair * 256 + 256)
+                qs = jnp.concatenate([q[:, hc] for hc in heads_of(kv, pair)], 0)
+                dos = jnp.concatenate([do[:, hc] for hc in heads_of(kv, pair)], 0)
+                scores = dot_nt(keys, qs) * EXP2_SCALE + bias[...]
+                top_own = stats[kv : kv + 1, at]
+                top = jnp.maximum(jnp.max(scores, axis=0, keepdims=True), top_own)
+                part = jnp.exp2(scores - top)
+                shift = jnp.exp2(top_own - top)
+                total = jnp.sum(part, axis=0, keepdims=True) + stats[4 + kv : 5 + kv, at] * shift
+                inverse = 1.0 / total
+                probs = part * inverse
+                weights = probs.astype(BF16)
+                factor = shift * inverse
+                weights_own = (lifted[kv, :, at] * factor).astype(BF16)
+                grad = dot_nt(values, dos)
+                delta = jnp.sum(
+                    weights.astype(F32) * grad + weights_own.astype(F32) * pgrad[kv, :, at],
+                    axis=0, keepdims=True,
+                )
+                score = (probs * (grad - delta)).astype(BF16)
+                ds[kv, :, at] = score
+                rowstats[kv : kv + 1, at] = factor
+                rowstats[4 + kv : 5 + kv, at] = delta
+                dv.append((weights, dos))
+                dk.append((score, qs))
+        for kv in kvs:
+            cols, vcols = cols_of(kv), cols_of(kv, KVW)
+            dv, dk = (joined_dot(t) for t in terms[kv])
+            for out, part in ((keep, slice(0, 64)), (send, slice(64, 128))):
+                out[odd, :, cols] += dk[part]
+                out[odd, :, vcols] += dv[part]
 
 
 def grad_kernel(
@@ -343,20 +349,16 @@
     )
 
 
-def prompt_part(slot, group, prompt_len, parts, near, far, after, before=()):
-    def kernel(*refs):
-        prompt_kernel(slot, *refs)
-
-    return call(
-        kernel, "ss" + "v" * 13 + "a" + "v" * len(before),
-        [group, prompt_len, *parts, *near, *far, after, *before],
-        [
-            ((KVH, PLEN, QW), BF16), ((8, QW), F32), ((PLEN, KVW), BF16),
-            ((2, 64, 2 * KVW), F32), ((2, 64, 2 * KVW), F32),
-        ],
-        scratch=[VMEM((PLEN, KVW), BF16), VMEM((PLEN, 2 * CLEN), F32)],
+def prompt_part(group, prompt_len, parts0, parts1, near, far, after):
+    scores = [((KVH, PLEN, QW), BF16), ((8, QW), F32), ((PLEN, KVW), BF16)]
+    outs = call(
+        prompt_kernel, "ss" + "v" * 18 + "a",
+        [group, prompt_len, *parts0, *parts1, *near, *far, after],
+        scores * 2 + [((2, 64, 2 * KVW), F32)] * 2,
+        scratch=[VMEM((COMP, PLEN, KVW), BF16), VMEM((COMP, PLEN, 2 * CLEN), F32)],
         limit=4,
     )
+    return outs[:3], outs[3:6], outs[6], outs[7]
 
 
 def grad_part(parts0, parts1, kown, scores0, scores1, after):
@@ -407,28 +409,25 @@
     far = [swap(x, 1) for x in near]
     (count,) = call(count_kernel, "v" * 8, [*near, *far], [((8, HD), F32)])
 
-    count1 = swap(count, 1, "grp")
-    *scores0, keep, send = prompt_part(
-        0, comp_group, prompt_len, parts0, near, far, count
-    )
-    count = count + count1
-    *scores1, keep, send = prompt_part(
-        1, comp_group, prompt_len, parts1, near, far, count, [keep, send]
-    )
-    got = swap(send, 1)
+    counts = [swap(count, 2 * m, "grp") for m in (1, 2, 3)]
+    scores0, scores1, keep, send = prompt_part(
+        comp_group, prompt_len, parts0, parts1, near, far, count
+    )
+    count = sum(counts, count)
+    got = swap(tie(send, [count]), 1)
     k0, s1, s2, s3 = call(
         chip_kernel, "vv", [keep, got],
         [((2, 16, wide), F32)] + [((2, 16, wide), BF16)] * 3,
     )
     got = [swap(s, 2 * (m + 1)) for m, s in enumerate((s1, s2, s3))]
     dq, own = grad_part(parts0, parts1, comp_key, scores0, scores1, k0)
-    count = count + swap(tie(count, [k0]), 2, "grp")
+    count = tie(count, [k0])
+    count = count + swap(count, 1, "grp")
     k1, s1, s2, s3 = call(
         sum_kernel, "vvvvvvaa", [near[0], far[0], k0, *got, own, count],
         [((16, wide), F32)] + [((16, wide), BF16)] * 3,
     )
     got = [swap(s, 8 * (m + 1)) for m, s in enumerate((s1, s2, s3))]
-    count = count + swap(tie(count, [k1]), 4, "grp")
     query_grad, comp_key_grad, comp_value_grad = scale_part(count, dq, own, k1)
     prompt_key_grad, prompt_value_grad = call(
         last_kernel, "vvvvv", [count, k1, *got], [((16, KVW), BF16)] * 2

time: 59.4 us -> 56.7 us (0.955)
  waiting for transfers between devices: 14.2 us -> 10.2 us
  starting transfers between devices: 26.4 us -> 28.6 us
  Pallas kernels: 17.7 us -> 16.8 us
    ppermute x20 -> x21, waiting for transfers between devices: 14.2 us -> 10.2 us  [swap(): lax.ppermute(x, axis, [(i, i ^ mask) for i in range(lax.axis_size(axis))])]
    ppermute x20 -> x21, starting transfers between devices: 26.4 us -> 28.6 us  [swap(): lax.ppermute(x, axis, [(i, i ^ mask) for i in range(lax.axis_size(axis))])]
    pallas_call x12 -> x11, Pallas kernels: 17.6 us -> 16.8 us  [call(): pl.pallas_call(kernel, out_shape=[jax.ShapeDtypeStruct(s, d) for s, d in...]
  transfers between devices with their start and end apart: 20 -> 21, of which waited for: 7 -> 7; matrix products, arithmetic and copies ran while one was open for 0% -> 0% of each run, Pallas kernels for 22% -> 27%
where the time goes in v2:
time: 56.7 us; the launch traced here: 56.5 us
  starting transfers between devices  28.6 us (50%)
  Pallas kernels  16.8 us (30%)
  waiting for transfers between devices  10.2 us (18%)
  between operations  0.83 us (1%)
    ppermute x21, starting transfers between devices, swap(): lax.ppermute(x, axis, [(i, i ^ mask) for i in range(lax.axis_size(axis))])  28.6 us
    pallas_call x11, Pallas kernels, call(): pl.pallas_call(kernel, out_shape=[jax.ShapeDtypeStruct(s, d) for s, d in...  16.8 us
    ppermute x21, waiting for transfers between devices, swap(): lax.ppermute(x, axis, [(i, i ^ mask) for i in range(lax.axis_size(axis))])  10.2 us
  transfers between devices with their start and end apart: 21, of which 7 were waited for; matrix products, arithmetic and copies ran while one was open for 0% of the time, Pallas kernels for 27%

profile of v2, /device:TPU:4, one launch (start us, length us, event | category | flops | bytes accessed | tf_op | source)
XLA Modules:
  0.0 56.5 jit_solution(6814288478987979839)
XLA Ops:
  0.6 0.8 %shard_map.128.refs_5_.c0 = bf16[16,1152]{1,0:T(8,128)(2,1)S(1)} custom-call(s32[2]{0:T(128)} %refs_0_.3, s32[2]{0:T(128)} %group.1, bf16[16,512]{1,0:T(8,128)(2,1)} %prompt_key.1, bf16[16,512]{1,0:T(8,128)(2,1)} %prompt_value.1), custom_call_target="tpu_custom_call" | custom-call | flops 1 | bytes 1 | tf_op jit(solution)/shard_map/pallas_call | solution.py:311
  1.4 4.7 %collective-permute-start.2 = (bf16[16,1152]{1,0:T(8,128)(2,1)S(1)}, bf16[16,1152]{1,0:T(8,128)(2,1)S(1)}, u32[]{:S(2)}, u32[]{:S(2)}) collective-permute-start(bf16[16,1152]{1,0:T(8,128)(2,1)S(1)} %shard_map.128.refs_5_.c0), channel_id=1, source_target_pairs={{0,6},{1,7},{2,4},{3,5},{4,2},{5,3},{6,0},{7,1},{8,14},{9,15},{10,... | collective-permute-start | bytes 110600 | tf_op jit(solution)/shard_map/ppermute | solution.py:387
  6.1 0.0 collective-permute-start.1
  6.1 0.7 %collective-permute-start = (bf16[16,1152]{1,0:T(8,128)(2,1)S(1)}, bf16[16,1152]{1,0:T(8,128)(2,1)S(1)}, u32[]{:S(2)}, u32[]{:S(2)}) collective-permute-start(bf16[16,1152]{1,0:T(8,128)(2,1)S(1)} %shard_map.128.refs_5_.c0), channel_id=1, source_target_pairs={{0,2},{1,3},{2,0},{3,1},{4,6},{5,7},{6,4},{7,5},{8,10},{9,11},{10,... | collective-permute-start | bytes 110600 | tf_op jit(solution)/shard_map/ppermute | solution.py:387
  6.8 2.7 %shard_map.129 = (bf16[128,4096]{1,0:T(8,128)(2,1)S(1)}, bf16[128,4096]{1,0:T(8,128)(2,1)S(1)}, f32[4,128,1024]{2,1,0:T(8,128)S(1)}, f32[4,128,1024]{2,1,0:T(8,128)S(1)}, f32[8,1024]{1,0:T(8,128)S(1)}) custom-call(s32[2]{0:T(128)} %refs_0_.3, bf16[256,4096]{1,0:T(8,128)(2,1)} %refs_1_.3, bf16[256,4096]{1,0:T(8,128)(2,1)} %refs_2_.3, bf16[256,512]{1,0:T(8,128)(2,1)} %kown.1, ...), custom_call_target="tpu_custom_call" | custom-call | flops 1 | bytes 1 | tf_op jit(solution)/shard_map/pallas_call | solution.py:311
  9.5 0.0 collective-permute-done.2.c3
  9.6 1.4 %collective-permute-done.1.c2 = bf16[16,1152]{1,0:T(8,128)(2,1)S(1)} collective-permute-done((bf16[16,1152]{1,0:T(8,128)(2,1)S(1)}, bf16[16,1152]{1,0:T(8,128)(2,1)S(1)}, u32[]{:S(2)}, u32[]{:S(2)}) %collective-permute-start.1) | collective-permute-done | bytes 36896 | tf_op jit(solution)/shard_map/ppermute | solution.py:387
  11.0 0.0 collective-permute-done.c1
  11.0 0.0 copy-start.1
  11.0 0.0 copy-start.2
  11.0 3.1 %collective-permute-start.5 = (bf16[64,1152]{1,0:T(8,128)(2,1)S(1)}, bf16[64,1152]{1,0:T(8,128)(2,1)S(1)}, u32[]{:S(2)}, u32[]{:S(2)}) collective-permute-start(bf16[64,1152]{1,0:T(8,128)(2,1)S(1)} %shard_map.130.refs_5_.o0.near), channel_id=1, source_target_pairs={{0,24},{1,25},{2,26},{3,27},{4,28},{5,29},{6,30},{7,31},{8,16},{9,... | collective-permute-start | bytes 442376 | tf_op jit(solution)/shard_map/ppermute | solution.py:387
  14.1 0.6 %collective-permute-start.4 = (bf16[64,1152]{1,0:T(8,128)(2,1)S(1)}, bf16[64,1152]{1,0:T(8,128)(2,1)S(1)}, u32[]{:S(2)}, u32[]{:S(2)}) collective-permute-start(bf16[64,1152]{1,0:T(8,128)(2,1)S(1)} %shard_map.130.refs_5_.o0.near), channel_id=1, source_target_pairs={{0,16},{1,17},{2,18},{3,19},{4,20},{5,21},{6,22},{7,23},{8,24},{9,... | collective-permute-start | bytes 442376 | tf_op jit(solution)/shard_map/ppermute | solution.py:387
  14.8 0.5 collective-permute-start.3
  15.2 0.0 collective-permute-start.6
  15.2 2.7 %shard_map.131 = (bf16[128,4096]{1,0:T(8,128)(2,1)S(1)}, bf16[128,4096]{1,0:T(8,128)(2,1)S(1)}, f32[4,128,1024]{2,1,0:T(8,128)S(1)}, f32[4,128,1024]{2,1,0:T(8,128)S(1)}, f32[8,1024]{1,0:T(8,128)S(1)}) custom-call(s32[2]{0:T(128)} %refs_0_.3, bf16[256,4096]{1,0:T(8,128)(2,1)} %refs_1_.3, bf16[256,4096]{1,0:T(8,128)(2,1)} %refs_2_.3, bf16[256,512]{1,0:T(8,128)(2,1)} %kown.1, ...), custom_call_target="tpu_custom_call" | custom-call | flops 1 | bytes 1 | tf_op jit(solution)/shard_map/pallas_call | solution.py:311
  18.0 1.5 %collective-permute-done.5.o3 = bf16[64,1152]{1,0:T(8,128)(2,1)S(1)} collective-permute-done((bf16[64,1152]{1,0:T(8,128)(2,1)S(1)}, bf16[64,1152]{1,0:T(8,128)(2,1)S(1)}, u32[]{:S(2)}, u32[]{:S(2)}) %collective-permute-start.5) | collective-permute-done | bytes 147488 | tf_op jit(solution)/shard_map/ppermute | solution.py:387
  19.5 0.0 collective-permute-start.9
  19.5 2.1 %collective-permute-done.4.o2 = bf16[64,1152]{1,0:T(8,128)(2,1)S(1)} collective-permute-done((bf16[64,1152]{1,0:T(8,128)(2,1)S(1)}, bf16[64,1152]{1,0:T(8,128)(2,1)S(1)}, u32[]{:S(2)}, u32[]{:S(2)}) %collective-permute-start.4) | collective-permute-done | bytes 147488 | tf_op jit(solution)/shard_map/ppermute | solution.py:387
  21.6 0.0 collective-permute-start.8
  21.6 0.0 collective-permute-done.3.refs_0_
  21.6 0.5 collective-permute-start.7
  22.2 0.0 collective-permute-done.6.t0.far
  22.2 0.0 collective-permute-done.9.t3
  22.2 0.8 %collective-permute-done.8.t2 = bf16[64,1152]{1,0:T(8,128)(2,1)S(1)} collective-permute-done((bf16[64,1152]{1,0:T(8,128)(2,1)S(1)}, bf16[64,1152]{1,0:T(8,128)(2,1)S(1)}, u32[]{:S(2)}, u32[]{:S(2)}) %collective-permute-start.8) | collective-permute-done | bytes 147488 | tf_op jit(solution)/shard_map/ppermute | solution.py:387
  23.0 0.2 collective-permute-done.7.t1
  23.3 0.6 %collective-permute-start.12 = (f32[8,128]{1,0:T(8,128)S(1)}, f32[8,128]{1,0:T(8,128)S(1)}, u32[]{:S(2)}, u32[]{:S(2)}) collective-permute-start(f32[8,128]{1,0:T(8,128)S(1)} %shard_map.133.after), channel_id=1, source_target_pairs={{0,192},{32,224},{64,128},{96,160},{128,64},{160,96},{192,0},{224,... | collective-permute-start | bytes 12296 | tf_op jit(solution)/shard_map/ppermute | solution.py:387
  23.9 2.7 %collective-permute-start.11 = (f32[8,128]{1,0:T(8,128)S(1)}, f32[8,128]{1,0:T(8,128)S(1)}, u32[]{:S(2)}, u32[]{:S(2)}) collective-permute-start(f32[8,128]{1,0:T(8,128)S(1)} %shard_map.133.after), channel_id=1, source_target_pairs={{0,128},{32,160},{64,192},{96,224},{128,0},{160,32},{192,64},{224,... | collective-permute-start | bytes 12296 | tf_op jit(solution)/shard_map/ppermute | solution.py:387
  26.6 0.8 %collective-permute-start.10 = (f32[8,128]{1,0:T(8,128)S(1)}, f32[8,128]{1,0:T(8,128)S(1)}, u32[]{:S(2)}, u32[]{:S(2)}) collective-permute-start(f32[8,128]{1,0:T(8,128)S(1)} %shard_map.133.after), channel_id=1, source_target_pairs={{0,64},{32,96},{64,0},{96,32},{128,192},{160,224},{192,128},{224,1... | collective-permute-start | bytes 12296 | tf_op jit(solution)/shard_map/ppermute | solution.py:387
  27.4 0.0 copy-done.1
  27.4 0.0 copy-done.2
  27.4 5.3 %shard_map.134 = (bf16[4,128,1024]{2,1,0:T(8,128)(2,1)S(1)}, f32[8,1024]{1,0:T(8,128)S(1)}, bf16[128,512]{1,0:T(8,128)(2,1)S(1)}, bf16[4,128,1024]{2,1,0:T(8,128...) custom-call(s32[2]{0:T(128)S(1)} %copy-done.1, ...), custom_call_target="tpu_custom_call" | custom-call | flops 1 | bytes 1 | tf_op jit(solution)/shard_map/pallas_call | solution.py:311
  32.7 0.0 copy-start
  32.8 0.0 collective-permute-done.12
  32.8 0.0 collective-permute-done.11
  32.8 0.0 collective-permute-done.10
  32.8 0.1 collective-permute-start.13
  32.9 1.9 %collective-permute-done.13.got = f32[2,64,1024]{2,1,0:T(8,128)S(1)} collective-permute-done((f32[2,64,1024]{2,1,0:T(8,128)S(1)}, f32[2,64,1024]{2,1,0:T(8,128)S(1)}, u32[]{:S(2)}, u32[]{:S(2)}) %collective-permute-start.13) | collective-permute-done | bytes 524320 | tf_op jit(solution)/shard_map/ppermute | solution.py:387
  34.8 0.1 shard_map.136
  34.9 0.4 collective-permute-start.15
  35.3 2.6 %collective-permute-start.16 = (bf16[2,16,1024]{2,1,0:T(8,128)(2,1)S(1)}, bf16[2,16,1024]{2,1,0:T(8,128)(2,1)S(1)}, u32[]{:S(2)}, u32[]{:S(2)}) collective-permute-start(bf16[2,16,1024]{2,1,0:T(8,128)(2,1)S(1)} %get-tuple-element.60), channel_id=1, source_target_pairs={{0,4},{1,5},{2,6},{3,7},{4,0},{5,1},{6,2},{7,3},{8,12},{9,13},{10,... | collective-permute-start | bytes 196616 | tf_op jit(solution)/shard_map/ppermute | solution.py:387
  37.9 1.4 %collective-permute-start.17 = (bf16[2,16,1024]{2,1,0:T(8,128)(2,1)S(1)}, bf16[2,16,1024]{2,1,0:T(8,128)(2,1)S(1)}, u32[]{:S(2)}, u32[]{:S(2)}) collective-permute-start(bf16[2,16,1024]{2,1,0:T(8,128)(2,1)S(1)} %get-tuple-element.61), channel_id=1, source_target_pairs={{0,6},{1,7},{2,4},{3,5},{4,2},{5,3},{6,0},{7,1},{8,14},{9,15},{10,... | collective-permute-start | bytes 196616 | tf_op jit(solution)/shard_map/ppermute | solution.py:387
  39.4 5.0 %collective-permute-start.14 = (f32[8,128]{1,0:T(8,128)S(1)}, f32[8,128]{1,0:T(8,128)S(1)}, u32[]{:S(2)}, u32[]{:S(2)}) collective-permute-start(f32[8,128]{1,0:T(8,128)S(1)} %shard_map.137), channel_id=1, source_target_pairs={{0,32},{32,0},{64,96},{96,64},{128,160},{160,128},{192,224},{224,1... | collective-permute-start | bytes 12296 | tf_op jit(solution)/shard_map/ppermute | solution.py:387
  44.3 0.0 copy-done
  44.3 2.7 %shard_map.138 = (f32[256,4096]{1,0:T(8,128)S(1)}, f32[256,1024]{1,0:T(8,128)S(1)}) custom-call(bf16[128,4096]{1,0:T(8,128)(2,1)S(1)} %get-tuple-element.40.q0, bf16[128,4096]{1,0:T(8,128)(2,1)S(1)} %get-tuple-element.41.do0, f32[4,128,1024]{2,1,0:T(8,128)S(1)} %get-tuple-element.42.e0, f32[4,128,1024]{2,1,0:T(8,128)S(1)} %get-tuple-element.43.g0, ...), custom_call_target="tpu_custom_call" | custom-call | flops 1 | bytes 1 | tf_op jit(solution)/shard_map/pallas_call | solution.py:311
  47.0 0.0 collective-permute-done.14
  47.1 0.0 collective-permute-done.15.r1
  47.1 0.0 collective-permute-done.16.r2
  47.1 0.0 collective-permute-done.17.r3
  47.1 0.1 shard_map.139
  47.2 0.5 collective-permute-start.18
  47.7 2.9 %collective-permute-start.19 = (bf16[16,1024]{1,0:T(8,128)(2,1)S(1)}, bf16[16,1024]{1,0:T(8,128)(2,1)S(1)}, u32[]{:S(2)}, u32[]{:S(2)}) collective-permute-start(bf16[16,1024]{1,0:T(8,128)(2,1)S(1)} %get-tuple-element.67), channel_id=1, source_target_pairs={{0,16},{1,17},{2,18},{3,19},{4,20},{5,21},{6,22},{7,23},{8,24},{9,... | collective-permute-start | bytes 98312 | tf_op jit(solution)/shard_map/ppermute | solution.py:387
  50.7 1.3 %collective-permute-start.20 = (bf16[16,1024]{1,0:T(8,128)(2,1)S(1)}, bf16[16,1024]{1,0:T(8,128)(2,1)S(1)}, u32[]{:S(2)}, u32[]{:S(2)}) collective-permute-start(bf16[16,1024]{1,0:T(8,128)(2,1)S(1)} %get-tuple-element.68), channel_id=1, source_target_pairs={{0,24},{1,25},{2,26},{3,27},{4,28},{5,29},{6,30},{7,31},{8,16},{9,... | collective-permute-start | bytes 98312 | tf_op jit(solution)/shard_map/ppermute | solution.py:387
  52.0 1.7 %shard_map.140 = (bf16[256,4096]{1,0:T(8,128)(2,1)}, bf16[256,512]{1,0:T(8,128)(2,1)}, bf16[256,512]{1,0:T(8,128)(2,1)}) custom-call(f32[8,128]{1,0:T(8,128)S(1)} %add.15.also.total, f32[256,4096]{1,0:T(8,128)S(1)} %get-tuple-element.57.dq, f32[256,1024]{1,0:T(8,128)S(1)} %get-tuple-element.58.after.own, f32[16,1024]{1,0:T(8,128)S(1)} %get-tuple-element.62.after.k1), custom_call_target="tpu_custom_call" | custom-call | flops 1 | bytes 1 | tf_op jit(solution)/shard_map/pallas_call | solution.py:311
  53.7 0.0 collective-permute-done.18.r1
  53.7 0.0 collective-permute-done.19.r2
  53.7 2.1 %collective-permute-done.20.r3 = bf16[16,1024]{1,0:T(8,128)(2,1)S(1)} collective-permute-done((bf16[16,1024]{1,0:T(8,128)(2,1)S(1)}, bf16[16,1024]{1,0:T(8,128)(2,1)S(1)}, u32[]{:S(2)}, u32[]{:S(2)}) %collective-permute-start.20) | collective-permute-done | bytes 32800 | tf_op jit(solution)/shard_map/ppermute | solution.py:387
  55.8 0.7 %shard_map.141 = (bf16[16,512]{1,0:T(8,128)(2,1)}, bf16[16,512]{1,0:T(8,128)(2,1)}) custom-call(f32[8,128]{1,0:T(8,128)S(1)} %add.15.also.total, f32[16,1024]{1,0:T(8,128)S(1)} %get-tuple-element.62.after.k1, bf16[16,1024]{1,0:T(8,128)(2,1)S(1)} %collective-permute-done.18.r1, bf16[16,1024]{1,0:T(8,128)(2,1)S(1)} %collective-permute-done.19.r2, ...), custom_call_target="tpu_custom_call" | custom-call | flops 1 | bytes 1 | tf_op jit(solution)/shard_map/pallas_call | solution.py:311
  (7 shorter events, 0.1 us)
Async XLA Ops:
  1.4 8.1 %collective-permute-start.2 = (bf16[16,1152]{1,0:T(8,128)(2,1)S(1)}, bf16[16,1152]{1,0:T(8,128)(2,1)S(1)}, u32[]{:S(2)}, u32[]{:S(2)}) collective-permute-start(bf16[16,1152]{1,0:T(8,128)(2,1)S(1)} %shard_map.128.refs_5_.c0), channel_id=1, source_target_pairs={{0,6},{1,7},{2,4},{3,5},{4,2},{5,3},{6,0},{7,1},{8,14},{9,15},{10,... | collective-permute-start | bytes 110600 | tf_op jit(solution)/shard_map/ppermute | solution.py:387
  6.1 4.9 %collective-permute-start.1 = (bf16[16,1152]{1,0:T(8,128)(2,1)S(1)}, bf16[16,1152]{1,0:T(8,128)(2,1)S(1)}, u32[]{:S(2)}, u32[]{:S(2)}) collective-permute-start(bf16[16,1152]{1,0:T(8,128)(2,1)S(1)} %shard_map.128.refs_5_.c0), channel_id=1, source_target_pairs={{0,4},{1,5},{2,6},{3,7},{4,0},{5,1},{6,2},{7,3},{8,12},{9,13},{10,... | collective-permute-start | bytes 110600 | tf_op jit(solution)/shard_map/ppermute | solution.py:387
  6.1 4.9 %collective-permute-start = (bf16[16,1152]{1,0:T(8,128)(2,1)S(1)}, bf16[16,1152]{1,0:T(8,128)(2,1)S(1)}, u32[]{:S(2)}, u32[]{:S(2)}) collective-permute-start(bf16[16,1152]{1,0:T(8,128)(2,1)S(1)} %shard_map.128.refs_5_.c0), channel_id=1, source_target_pairs={{0,2},{1,3},{2,0},{3,1},{4,6},{5,7},{6,4},{7,5},{8,10},{9,11},{10,... | collective-permute-start | bytes 110600 | tf_op jit(solution)/shard_map/ppermute | solution.py:387
  11.0 16.4 %copy-start.1 = (s32[2]{0:T(128)S(1)}, s32[2]{0:T(128)}, u32[]{:S(2)}) copy-start(s32[2]{0:T(128)} %group.1) | copy-start | bytes 28
  11.0 16.4 %copy-start.2 = (s32[4]{0:T(128)S(1)}, s32[4]{0:T(128)}, u32[]{:S(2)}) copy-start(s32[4]{0:T(128)} %prompt_len.1) | copy-start | bytes 52
  11.0 8.5 %collective-permute-start.5 = (bf16[64,1152]{1,0:T(8,128)(2,1)S(1)}, bf16[64,1152]{1,0:T(8,128)(2,1)S(1)}, u32[]{:S(2)}, u32[]{:S(2)}) collective-permute-start(bf16[64,1152]{1,0:T(8,128)(2,1)S(1)} %shard_map.130.refs_5_.o0.near), channel_id=1, source_target_pairs={{0,24},{1,25},{2,26},{3,27},{4,28},{5,29},{6,30},{7,31},{8,16},{9,... | collective-permute-start | bytes 442376 | tf_op jit(solution)/shard_map/ppermute | solution.py:387
  14.1 7.5 %collective-permute-start.4 = (bf16[64,1152]{1,0:T(8,128)(2,1)S(1)}, bf16[64,1152]{1,0:T(8,128)(2,1)S(1)}, u32[]{:S(2)}, u32[]{:S(2)}) collective-permute-start(bf16[64,1152]{1,0:T(8,128)(2,1)S(1)} %shard_map.130.refs_5_.o0.near), channel_id=1, source_target_pairs={{0,16},{1,17},{2,18},{3,19},{4,20},{5,21},{6,22},{7,23},{8,24},{9,... | collective-permute-start | bytes 442376 | tf_op jit(solution)/shard_map/ppermute | solution.py:387
  14.8 6.9 %collective-permute-start.3 = (bf16[64,1152]{1,0:T(8,128)(2,1)S(1)}, bf16[64,1152]{1,0:T(8,128)(2,1)S(1)}, u32[]{:S(2)}, u32[]{:S(2)}) collective-permute-start(bf16[64,1152]{1,0:T(8,128)(2,1)S(1)} %shard_map.130.refs_5_.o0.near), channel_id=1, source_target_pairs={{0,8},{1,9},{2,10},{3,11},{4,12},{5,13},{6,14},{7,15},{8,0},{9,1},... | collective-permute-start | bytes 442376 | tf_op jit(solution)/shard_map/ppermute | solution.py:387
  15.2 7.0 %collective-permute-start.6 = (bf16[64,1152]{1,0:T(8,128)(2,1)S(1)}, bf16[64,1152]{1,0:T(8,128)(2,1)S(1)}, u32[]{:S(2)}, u32[]{:S(2)}) collective-permute-start(bf16[64,1152]{1,0:T(8,128)(2,1)S(1)} %shard_map.130.refs_5_.o0.near), channel_id=1, source_target_pairs={{0,1},{1,0},{2,3},{3,2},{4,5},{5,4},{6,7},{7,6},{8,9},{9,8},{10,11... | collective-permute-start | bytes 442376 | tf_op jit(solution)/shard_map/ppermute | solution.py:387
  19.5 2.7 %collective-permute-start.9 = (bf16[64,1152]{1,0:T(8,128)(2,1)S(1)}, bf16[64,1152]{1,0:T(8,128)(2,1)S(1)}, u32[]{:S(2)}, u32[]{:S(2)}) collective-permute-start(bf16[64,1152]{1,0:T(8,128)(2,1)S(1)} %collective-permute-done.5.o3), channel_id=1, source_target_pairs={{0,1},{1,0},{2,3},{3,2},{4,5},{5,4},{6,7},{7,6},{8,9},{9,8},{10,11... | collective-permute-start | bytes 442376 | tf_op jit(solution)/shard_map/ppermute | solution.py:387
  21.6 1.4 %collective-permute-start.8 = (bf16[64,1152]{1,0:T(8,128)(2,1)S(1)}, bf16[64,1152]{1,0:T(8,128)(2,1)S(1)}, u32[]{:S(2)}, u32[]{:S(2)}) collective-permute-start(bf16[64,1152]{1,0:T(8,128)(2,1)S(1)} %collective-permute-done.4.o2), channel_id=1, source_target_pairs={{0,1},{1,0},{2,3},{3,2},{4,5},{5,4},{6,7},{7,6},{8,9},{9,8},{10,11... | collective-permute-start | bytes 442376 | tf_op jit(solution)/shard_map/ppermute | solution.py:387
  21.6 1.6 %collective-permute-start.7 = (bf16[64,1152]{1,0:T(8,128)(2,1)S(1)}, bf16[64,1152]{1,0:T(8,128)(2,1)S(1)}, u32[]{:S(2)}, u32[]{:S(2)}) collective-permute-start(bf16[64,1152]{1,0:T(8,128)(2,1)S(1)} %shard_map.132.o1), channel_id=1, source_target_pairs={{0,1},{1,0},{2,3},{3,2},{4,5},{5,4},{6,7},{7,6},{8,9},{9,8},{10,11... | collective-permute-start | bytes 442376 | tf_op jit(solution)/shard_map/ppermute | solution.py:387
  23.3 9.5 %collective-permute-start.12 = (f32[8,128]{1,0:T(8,128)S(1)}, f32[8,128]{1,0:T(8,128)S(1)}, u32[]{:S(2)}, u32[]{:S(2)}) collective-permute-start(f32[8,128]{1,0:T(8,128)S(1)} %shard_map.133.after), channel_id=1, source_target_pairs={{0,192},{32,224},{64,128},{96,160},{128,64},{160,96},{192,0},{224,... | collective-permute-start | bytes 12296 | tf_op jit(solution)/shard_map/ppermute | solution.py:387
  23.9 8.9 %collective-permute-start.11 = (f32[8,128]{1,0:T(8,128)S(1)}, f32[8,128]{1,0:T(8,128)S(1)}, u32[]{:S(2)}, u32[]{:S(2)}) collective-permute-start(f32[8,128]{1,0:T(8,128)S(1)} %shard_map.133.after), channel_id=1, source_target_pairs={{0,128},{32,160},{64,192},{96,224},{128,0},{160,32},{192,64},{224,... | collective-permute-start | bytes 12296 | tf_op jit(solution)/shard_map/ppermute | solution.py:387
  26.6 6.2 %collective-permute-start.10 = (f32[8,128]{1,0:T(8,128)S(1)}, f32[8,128]{1,0:T(8,128)S(1)}, u32[]{:S(2)}, u32[]{:S(2)}) collective-permute-start(f32[8,128]{1,0:T(8,128)S(1)} %shard_map.133.after), channel_id=1, source_target_pairs={{0,64},{32,96},{64,0},{96,32},{128,192},{160,224},{192,128},{224,1... | collective-permute-start | bytes 12296 | tf_op jit(solution)/shard_map/ppermute | solution.py:387
  32.7 11.6 %copy-start = (bf16[256,512]{1,0:T(8,128)(2,1)S(1)}, bf16[256,512]{1,0:T(8,128)(2,1)}, u32[]{:S(2)}) copy-start(bf16[256,512]{1,0:T(8,128)(2,1)} %kown.1) | copy-start | bytes 786436
  32.8 2.0 %collective-permute-start.13 = (f32[2,64,1024]{2,1,0:T(8,128)S(1)}, f32[2,64,1024]{2,1,0:T(8,128)S(1)}, u32[]{:S(2)}, u32[]{:S(2)}) collective-permute-start(f32[2,64,1024]{2,1,0:T(8,128)S(1)} %shard_map.135), channel_id=1, source_target_pairs={{0,1},{1,0},{2,3},{3,2},{4,5},{5,4},{6,7},{7,6},{8,9},{9,8},{10,11... | collective-permute-start | bytes 1572872 | tf_op jit(solution)/shard_map/ppermute | solution.py:387
  34.9 12.2 %collective-permute-start.15 = (bf16[2,16,1024]{2,1,0:T(8,128)(2,1)S(1)}, bf16[2,16,1024]{2,1,0:T(8,128)(2,1)S(1)}, u32[]{:S(2)}, u32[]{:S(2)}) collective-permute-start(bf16[2,16,1024]{2,1,0:T(8,128)(2,1)S(1)} %get-tuple-element.59), channel_id=1, source_target_pairs={{0,2},{1,3},{2,0},{3,1},{4,6},{5,7},{6,4},{7,5},{8,10},{9,11},{10,... | collective-permute-start | bytes 196616 | tf_op jit(solution)/shard_map/ppermute | solution.py:387
  35.3 11.8 %collective-permute-start.16 = (bf16[2,16,1024]{2,1,0:T(8,128)(2,1)S(1)}, bf16[2,16,1024]{2,1,0:T(8,128)(2,1)S(1)}, u32[]{:S(2)}, u32[]{:S(2)}) collective-permute-start(bf16[2,16,1024]{2,1,0:T(8,128)(2,1)S(1)} %get-tuple-element.60), channel_id=1, source_target_pairs={{0,4},{1,5},{2,6},{3,7},{4,0},{5,1},{6,2},{7,3},{8,12},{9,13},{10,... | collective-permute-start | bytes 196616 | tf_op jit(solution)/shard_map/ppermute | solution.py:387
  37.9 9.1 %collective-permute-start.17 = (bf16[2,16,1024]{2,1,0:T(8,128)(2,1)S(1)}, bf16[2,16,1024]{2,1,0:T(8,128)(2,1)S(1)}, u32[]{:S(2)}, u32[]{:S(2)}) collective-permute-start(bf16[2,16,1024]{2,1,0:T(8,128)(2,1)S(1)} %get-tuple-element.61), channel_id=1, source_target_pairs={{0,6},{1,7},{2,4},{3,5},{4,2},{5,3},{6,0},{7,1},{8,14},{9,15},{10,... | collective-permute-start | bytes 196616 | tf_op jit(solution)/shard_map/ppermute | solution.py:387
  39.4 7.7 %collective-permute-start.14 = (f32[8,128]{1,0:T(8,128)S(1)}, f32[8,128]{1,0:T(8,128)S(1)}, u32[]{:S(2)}, u32[]{:S(2)}) collective-permute-start(f32[8,128]{1,0:T(8,128)S(1)} %shard_map.137), channel_id=1, source_target_pairs={{0,32},{32,0},{64,96},{96,64},{128,160},{160,128},{192,224},{224,1... | collective-permute-start | bytes 12296 | tf_op jit(solution)/shard_map/ppermute | solution.py:387
  47.2 6.5 %collective-permute-start.18 = (bf16[16,1024]{1,0:T(8,128)(2,1)S(1)}, bf16[16,1024]{1,0:T(8,128)(2,1)S(1)}, u32[]{:S(2)}, u32[]{:S(2)}) collective-permute-start(bf16[16,1024]{1,0:T(8,128)(2,1)S(1)} %get-tuple-element.66), channel_id=1, source_target_pairs={{0,8},{1,9},{2,10},{3,11},{4,12},{5,13},{6,14},{7,15},{8,0},{9,1},... | collective-permute-start | bytes 98312 | tf_op jit(solution)/shard_map/ppermute | solution.py:387
  47.7 6.0 %collective-permute-start.19 = (bf16[16,1024]{1,0:T(8,128)(2,1)S(1)}, bf16[16,1024]{1,0:T(8,128)(2,1)S(1)}, u32[]{:S(2)}, u32[]{:S(2)}) collective-permute-start(bf16[16,1024]{1,0:T(8,128)(2,1)S(1)} %get-tuple-element.67), channel_id=1, source_target_pairs={{0,16},{1,17},{2,18},{3,19},{4,20},{5,21},{6,22},{7,23},{8,24},{9,... | collective-permute-start | bytes 98312 | tf_op jit(solution)/shard_map/ppermute | solution.py:387
  50.7 5.1 %collective-permute-start.20 = (bf16[16,1024]{1,0:T(8,128)(2,1)S(1)}, bf16[16,1024]{1,0:T(8,128)(2,1)S(1)}, u32[]{:S(2)}, u32[]{:S(2)}) collective-permute-start(bf16[16,1024]{1,0:T(8,128)(2,1)S(1)} %get-tuple-element.68), channel_id=1, source_target_pairs={{0,24},{1,25},{2,26},{3,27},{4,28},{5,29},{6,30},{7,31},{8,16},{9,... | collective-permute-start | bytes 98312 | tf_op jit(solution)/shard_map/ppermute | solution.py:387

commit v3 on v2

--- a/solution.py
+++ b/solution.py
@@ -419,7 +419,7 @@
         chip_kernel, "vv", [keep, got],
         [((2, 16, wide), F32)] + [((2, 16, wide), BF16)] * 3,
     )
-    got = [swap(s, 2 * (m + 1)) for m, s in enumerate((s1, s2, s3))]
+    got = [swap(s, 2 * m) for m, s in ((3, s3), (2, s2), (1, s1))]
     dq, own = grad_part(parts0, parts1, comp_key, scores0, scores1, k0)
     count = tie(count, [k0])
     count = count + swap(count, 1, "grp")
@@ -427,7 +427,7 @@
         sum_kernel, "vvvvvvaa", [near[0], far[0], k0, *got, own, count],
         [((16, wide), F32)] + [((16, wide), BF16)] * 3,
     )
-    got = [swap(s, 8 * (m + 1)) for m, s in enumerate((s1, s2, s3))]
+    got = [swap(s, 8 * m) for m, s in ((2, s2), (3, s3), (1, s1))]
     query_grad, comp_key_grad, comp_value_grad = scale_part(count, dq, own, k1)
     prompt_key_grad, prompt_value_grad = call(
         last_kernel, "vvvvv", [count, k1, *got], [((16, KVW), BF16)] * 2

time: 56.7 us -> 55.4 us (0.977)
  starting transfers between devices: 28.6 us -> 27.4 us
    ppermute x21, starting transfers between devices: 28.6 us -> 27.4 us  [swap(): lax.ppermute(x, axis, [(i, i ^ mask) for i in range(lax.axis_size(axis))])]
  transfers between devices with their start and end apart: 21 -> 21, of which waited for: 7 -> 8; matrix products, arithmetic and copies ran while one was open for 0% -> 0% of each run, Pallas kernels for 27% -> 27%
where the time goes in v3:
time: 55.4 us; the launch traced here: 55.2 us
  starting transfers between devices  27.4 us (49%)
  Pallas kernels  16.8 us (30%)
  waiting for transfers between devices  10.2 us (18%)
  between operations  0.82 us (1%)
    ppermute x21, starting transfers between devices, swap(): lax.ppermute(x, axis, [(i, i ^ mask) for i in range(lax.axis_size(axis))])  27.4 us
    pallas_call x11, Pallas kernels, call(): pl.pallas_call(kernel, out_shape=[jax.ShapeDtypeStruct(s, d) for s, d in...  16.8 us
    ppermute x21, waiting for transfers between devices, swap(): lax.ppermute(x, axis, [(i, i ^ mask) for i in range(lax.axis_size(axis))])  10.2 us
  transfers between devices with their start and end apart: 21, of which 8 were waited for; matrix products, arithmetic and copies ran while one was open for 0% of the time, Pallas kernels for 27%

profile of v3, /device:TPU:4, one launch (start us, length us, event | category | flops | bytes accessed | tf_op | source)
XLA Modules:
  0.0 55.2 jit_solution(11862333932244190012)
XLA Ops:
  0.6 0.8 %shard_map.128.refs_5_.c0 = bf16[16,1152]{1,0:T(8,128)(2,1)S(1)} custom-call(s32[2]{0:T(128)} %refs_0_.3, s32[2]{0:T(128)} %group.1, bf16[16,512]{1,0:T(8,128)(2,1)} %prompt_key.1, bf16[16,512]{1,0:T(8,128)(2,1)} %prompt_value.1), custom_call_target="tpu_custom_call" | custom-call | flops 1 | bytes 1 | tf_op jit(solution)/shard_map/pallas_call | solution.py:311
  1.4 4.7 %collective-permute-start.2 = (bf16[16,1152]{1,0:T(8,128)(2,1)S(1)}, bf16[16,1152]{1,0:T(8,128)(2,1)S(1)}, u32[]{:S(2)}, u32[]{:S(2)}) collective-permute-start(bf16[16,1152]{1,0:T(8,128)(2,1)S(1)} %shard_map.128.refs_5_.c0), channel_id=1, source_target_pairs={{0,6},{1,7},{2,4},{3,5},{4,2},{5,3},{6,0},{7,1},{8,14},{9,15},{10,... | collective-permute-start | bytes 110600 | tf_op jit(solution)/shard_map/ppermute | solution.py:387
  6.1 0.0 collective-permute-start.1
  6.1 0.7 %collective-permute-start = (bf16[16,1152]{1,0:T(8,128)(2,1)S(1)}, bf16[16,1152]{1,0:T(8,128)(2,1)S(1)}, u32[]{:S(2)}, u32[]{:S(2)}) collective-permute-start(bf16[16,1152]{1,0:T(8,128)(2,1)S(1)} %shard_map.128.refs_5_.c0), channel_id=1, source_target_pairs={{0,2},{1,3},{2,0},{3,1},{4,6},{5,7},{6,4},{7,5},{8,10},{9,11},{10,... | collective-permute-start | bytes 110600 | tf_op jit(solution)/shard_map/ppermute | solution.py:387
  6.8 2.7 %shard_map.129 = (bf16[128,4096]{1,0:T(8,128)(2,1)S(1)}, bf16[128,4096]{1,0:T(8,128)(2,1)S(1)}, f32[4,128,1024]{2,1,0:T(8,128)S(1)}, f32[4,128,1024]{2,1,0:T(8,128)S(1)}, f32[8,1024]{1,0:T(8,128)S(1)}) custom-call(s32[2]{0:T(128)} %refs_0_.3, bf16[256,4096]{1,0:T(8,128)(2,1)} %refs_1_.3, bf16[256,4096]{1,0:T(8,128)(2,1)} %refs_2_.3, bf16[256,512]{1,0:T(8,128)(2,1)} %kown.1, ...), custom_call_target="tpu_custom_call" | custom-call | flops 1 | bytes 1 | tf_op jit(solution)/shard_map/pallas_call | solution.py:311
  9.5 0.0 collective-permute-done.2.c3
  9.6 1.4 %collective-permute-done.1.c2 = bf16[16,1152]{1,0:T(8,128)(2,1)S(1)} collective-permute-done((bf16[16,1152]{1,0:T(8,128)(2,1)S(1)}, bf16[16,1152]{1,0:T(8,128)(2,1)S(1)}, u32[]{:S(2)}, u32[]{:S(2)}) %collective-permute-start.1) | collective-permute-done | bytes 36896 | tf_op jit(solution)/shard_map/ppermute | solution.py:387
  11.0 0.0 collective-permute-done.c1
  11.0 0.0 copy-start.1
  11.0 0.0 copy-start.2
  11.0 3.1 %collective-permute-start.5 = (bf16[64,1152]{1,0:T(8,128)(2,1)S(1)}, bf16[64,1152]{1,0:T(8,128)(2,1)S(1)}, u32[]{:S(2)}, u32[]{:S(2)}) collective-permute-start(bf16[64,1152]{1,0:T(8,128)(2,1)S(1)} %shard_map.130.refs_5_.o0.near), channel_id=1, source_target_pairs={{0,24},{1,25},{2,26},{3,27},{4,28},{5,29},{6,30},{7,31},{8,16},{9,... | collective-permute-start | bytes 442376 | tf_op jit(solution)/shard_map/ppermute | solution.py:387
  14.1 0.6 %collective-permute-start.4 = (bf16[64,1152]{1,0:T(8,128)(2,1)S(1)}, bf16[64,1152]{1,0:T(8,128)(2,1)S(1)}, u32[]{:S(2)}, u32[]{:S(2)}) collective-permute-start(bf16[64,1152]{1,0:T(8,128)(2,1)S(1)} %shard_map.130.refs_5_.o0.near), channel_id=1, source_target_pairs={{0,16},{1,17},{2,18},{3,19},{4,20},{5,21},{6,22},{7,23},{8,24},{9,... | collective-permute-start | bytes 442376 | tf_op jit(solution)/shard_map/ppermute | solution.py:387
  14.8 0.5 collective-permute-start.3
  15.2 0.0 collective-permute-start.6
  15.2 2.7 %shard_map.131 = (bf16[128,4096]{1,0:T(8,128)(2,1)S(1)}, bf16[128,4096]{1,0:T(8,128)(2,1)S(1)}, f32[4,128,1024]{2,1,0:T(8,128)S(1)}, f32[4,128,1024]{2,1,0:T(8,128)S(1)}, f32[8,1024]{1,0:T(8,128)S(1)}) custom-call(s32[2]{0:T(128)} %refs_0_.3, bf16[256,4096]{1,0:T(8,128)(2,1)} %refs_1_.3, bf16[256,4096]{1,0:T(8,128)(2,1)} %refs_2_.3, bf16[256,512]{1,0:T(8,128)(2,1)} %kown.1, ...), custom_call_target="tpu_custom_call" | custom-call | flops 1 | bytes 1 | tf_op jit(solution)/shard_map/pallas_call | solution.py:311
  18.0 1.5 %collective-permute-done.5.o3 = bf16[64,1152]{1,0:T(8,128)(2,1)S(1)} collective-permute-done((bf16[64,1152]{1,0:T(8,128)(2,1)S(1)}, bf16[64,1152]{1,0:T(8,128)(2,1)S(1)}, u32[]{:S(2)}, u32[]{:S(2)}) %collective-permute-start.5) | collective-permute-done | bytes 147488 | tf_op jit(solution)/shard_map/ppermute | solution.py:387
  19.5 0.0 collective-permute-start.9
  19.5 2.1 %collective-permute-done.4.o2 = bf16[64,1152]{1,0:T(8,128)(2,1)S(1)} collective-permute-done((bf16[64,1152]{1,0:T(8,128)(2,1)S(1)}, bf16[64,1152]{1,0:T(8,128)(2,1)S(1)}, u32[]{:S(2)}, u32[]{:S(2)}) %collective-permute-start.4) | collective-permute-done | bytes 147488 | tf_op jit(solution)/shard_map/ppermute | solution.py:387
  21.6 0.0 collective-permute-start.8
  21.6 0.0 collective-permute-done.3.refs_0_
  21.6 0.5 collective-permute-start.7
  22.2 0.0 collective-permute-done.6.t0.far
  22.2 0.0 collective-permute-done.9.t3
  22.2 0.8 %collective-permute-done.8.t2 = bf16[64,1152]{1,0:T(8,128)(2,1)S(1)} collective-permute-done((bf16[64,1152]{1,0:T(8,128)(2,1)S(1)}, bf16[64,1152]{1,0:T(8,128)(2,1)S(1)}, u32[]{:S(2)}, u32[]{:S(2)}) %collective-permute-start.8) | collective-permute-done | bytes 147488 | tf_op jit(solution)/shard_map/ppermute | solution.py:387
  23.0 0.2 collective-permute-done.7.t1
  23.3 0.6 %collective-permute-start.12 = (f32[8,128]{1,0:T(8,128)S(1)}, f32[8,128]{1,0:T(8,128)S(1)}, u32[]{:S(2)}, u32[]{:S(2)}) collective-permute-start(f32[8,128]{1,0:T(8,128)S(1)} %shard_map.133.after), channel_id=1, source_target_pairs={{0,192},{32,224},{64,128},{96,160},{128,64},{160,96},{192,0},{224,... | collective-permute-start | bytes 12296 | tf_op jit(solution)/shard_map/ppermute | solution.py:387
  23.9 2.7 %collective-permute-start.11 = (f32[8,128]{1,0:T(8,128)S(1)}, f32[8,128]{1,0:T(8,128)S(1)}, u32[]{:S(2)}, u32[]{:S(2)}) collective-permute-start(f32[8,128]{1,0:T(8,128)S(1)} %shard_map.133.after), channel_id=1, source_target_pairs={{0,128},{32,160},{64,192},{96,224},{128,0},{160,32},{192,64},{224,... | collective-permute-start | bytes 12296 | tf_op jit(solution)/shard_map/ppermute | solution.py:387
  26.6 0.8 %collective-permute-start.10 = (f32[8,128]{1,0:T(8,128)S(1)}, f32[8,128]{1,0:T(8,128)S(1)}, u32[]{:S(2)}, u32[]{:S(2)}) collective-permute-start(f32[8,128]{1,0:T(8,128)S(1)} %shard_map.133.after), channel_id=1, source_target_pairs={{0,64},{32,96},{64,0},{96,32},{128,192},{160,224},{192,128},{224,1... | collective-permute-start | bytes 12296 | tf_op jit(solution)/shard_map/ppermute | solution.py:387
  27.4 0.0 copy-done.1
  27.4 0.0 copy-done.2
  27.4 5.3 %shard_map.134 = (bf16[4,128,1024]{2,1,0:T(8,128)(2,1)S(1)}, f32[8,1024]{1,0:T(8,128)S(1)}, bf16[128,512]{1,0:T(8,128)(2,1)S(1)}, bf16[4,128,1024]{2,1,0:T(8,128...) custom-call(s32[2]{0:T(128)S(1)} %copy-done.1, ...), custom_call_target="tpu_custom_call" | custom-call | flops 1 | bytes 1 | tf_op jit(solution)/shard_map/pallas_call | solution.py:311
  32.7 0.0 copy-start
  32.8 0.0 collective-permute-done.12
  32.8 0.0 collective-permute-done.11
  32.8 0.0 collective-permute-done.10
  32.8 0.1 collective-permute-start.13
  32.9 1.9 %collective-permute-done.13.got = f32[2,64,1024]{2,1,0:T(8,128)S(1)} collective-permute-done((f32[2,64,1024]{2,1,0:T(8,128)S(1)}, f32[2,64,1024]{2,1,0:T(8,128)S(1)}, u32[]{:S(2)}, u32[]{:S(2)}) %collective-permute-start.13) | collective-permute-done | bytes 524320 | tf_op jit(solution)/shard_map/ppermute | solution.py:387
  34.8 0.1 shard_map.136
  34.9 2.5 %collective-permute-start.15 = (bf16[2,16,1024]{2,1,0:T(8,128)(2,1)S(1)}, bf16[2,16,1024]{2,1,0:T(8,128)(2,1)S(1)}, u32[]{:S(2)}, u32[]{:S(2)}) collective-permute-start(bf16[2,16,1024]{2,1,0:T(8,128)(2,1)S(1)} %get-tuple-element.59), channel_id=1, source_target_pairs={{0,6},{1,7},{2,4},{3,5},{4,2},{5,3},{6,0},{7,1},{8,14},{9,15},{10,... | collective-permute-start | bytes 196616 | tf_op jit(solution)/shard_map/ppermute | solution.py:387
  37.4 0.0 collective-permute-start.16
  37.4 2.0 %collective-permute-start.17 = (bf16[2,16,1024]{2,1,0:T(8,128)(2,1)S(1)}, bf16[2,16,1024]{2,1,0:T(8,128)(2,1)S(1)}, u32[]{:S(2)}, u32[]{:S(2)}) collective-permute-start(bf16[2,16,1024]{2,1,0:T(8,128)(2,1)S(1)} %get-tuple-element.61), channel_id=1, source_target_pairs={{0,2},{1,3},{2,0},{3,1},{4,6},{5,7},{6,4},{7,5},{8,10},{9,11},{10,... | collective-permute-start | bytes 196616 | tf_op jit(solution)/shard_map/ppermute | solution.py:387
  39.4 5.0 %collective-permute-start.14 = (f32[8,128]{1,0:T(8,128)S(1)}, f32[8,128]{1,0:T(8,128)S(1)}, u32[]{:S(2)}, u32[]{:S(2)}) collective-permute-start(f32[8,128]{1,0:T(8,128)S(1)} %shard_map.137), channel_id=1, source_target_pairs={{0,32},{32,0},{64,96},{96,64},{128,160},{160,128},{192,224},{224,1... | collective-permute-start | bytes 12296 | tf_op jit(solution)/shard_map/ppermute | solution.py:387
  44.3 0.0 copy-done
  44.3 2.7 %shard_map.138 = (f32[256,4096]{1,0:T(8,128)S(1)}, f32[256,1024]{1,0:T(8,128)S(1)}) custom-call(bf16[128,4096]{1,0:T(8,128)(2,1)S(1)} %get-tuple-element.40.q0, bf16[128,4096]{1,0:T(8,128)(2,1)S(1)} %get-tuple-element.41.do0, f32[4,128,1024]{2,1,0:T(8,128)S(1)} %get-tuple-element.42.e0, f32[4,128,1024]{2,1,0:T(8,128)S(1)} %get-tuple-element.43.g0, ...), custom_call_target="tpu_custom_call" | custom-call | flops 1 | bytes 1 | tf_op jit(solution)/shard_map/pallas_call | solution.py:311
  47.0 0.0 collective-permute-done.14
  47.1 0.0 collective-permute-done.15.r1
  47.1 0.0 collective-permute-done.16.r2
  47.1 0.0 collective-permute-done.17.r3
  47.1 0.1 shard_map.139
  47.2 2.2 %collective-permute-start.18 = (bf16[16,1024]{1,0:T(8,128)(2,1)S(1)}, bf16[16,1024]{1,0:T(8,128)(2,1)S(1)}, u32[]{:S(2)}, u32[]{:S(2)}) collective-permute-start(bf16[16,1024]{1,0:T(8,128)(2,1)S(1)} %get-tuple-element.66), channel_id=1, source_target_pairs={{0,16},{1,17},{2,18},{3,19},{4,20},{5,21},{6,22},{7,23},{8,24},{9,... | collective-permute-start | bytes 98312 | tf_op jit(solution)/shard_map/ppermute | solution.py:387
  49.4 1.0 %collective-permute-start.19 = (bf16[16,1024]{1,0:T(8,128)(2,1)S(1)}, bf16[16,1024]{1,0:T(8,128)(2,1)S(1)}, u32[]{:S(2)}, u32[]{:S(2)}) collective-permute-start(bf16[16,1024]{1,0:T(8,128)(2,1)S(1)} %get-tuple-element.67), channel_id=1, source_target_pairs={{0,24},{1,25},{2,26},{3,27},{4,28},{5,29},{6,30},{7,31},{8,16},{9,... | collective-permute-start | bytes 98312 | tf_op jit(solution)/shard_map/ppermute | solution.py:387
  50.4 0.4 collective-permute-start.20
  50.8 1.7 %shard_map.140 = (bf16[256,4096]{1,0:T(8,128)(2,1)}, bf16[256,512]{1,0:T(8,128)(2,1)}, bf16[256,512]{1,0:T(8,128)(2,1)}) custom-call(f32[8,128]{1,0:T(8,128)S(1)} %add.15.also.total, f32[256,4096]{1,0:T(8,128)S(1)} %get-tuple-element.57.dq, f32[256,1024]{1,0:T(8,128)S(1)} %get-tuple-element.58.after.own, f32[16,1024]{1,0:T(8,128)S(1)} %get-tuple-element.62.after.k1), custom_call_target="tpu_custom_call" | custom-call | flops 1 | bytes 1 | tf_op jit(solution)/shard_map/pallas_call | solution.py:311
  52.5 0.2 collective-permute-done.18.r1
  52.7 1.8 %collective-permute-done.19.r2 = bf16[16,1024]{1,0:T(8,128)(2,1)S(1)} collective-permute-done((bf16[16,1024]{1,0:T(8,128)(2,1)S(1)}, bf16[16,1024]{1,0:T(8,128)(2,1)S(1)}, u32[]{:S(2)}, u32[]{:S(2)}) %collective-permute-start.19) | collective-permute-done | bytes 32800 | tf_op jit(solution)/shard_map/ppermute | solution.py:387
  54.5 0.0 collective-permute-done.20.r3
  54.5 0.7 %shard_map.141 = (bf16[16,512]{1,0:T(8,128)(2,1)}, bf16[16,512]{1,0:T(8,128)(2,1)}) custom-call(f32[8,128]{1,0:T(8,128)S(1)} %add.15.also.total, f32[16,1024]{1,0:T(8,128)S(1)} %get-tuple-element.62.after.k1, bf16[16,1024]{1,0:T(8,128)(2,1)S(1)} %collective-permute-done.18.r1, bf16[16,1024]{1,0:T(8,128)(2,1)S(1)} %collective-permute-done.19.r2, ...), custom_call_target="tpu_custom_call" | custom-call | flops 1 | bytes 1 | tf_op jit(solution)/shard_map/pallas_call | solution.py:311
  (7 shorter events, 0.1 us)
Async XLA Ops:
  1.4 8.1 %collective-permute-start.2 = (bf16[16,1152]{1,0:T(8,128)(2,1)S(1)}, bf16[16,1152]{1,0:T(8,128)(2,1)S(1)}, u32[]{:S(2)}, u32[]{:S(2)}) collective-permute-start(bf16[16,1152]{1,0:T(8,128)(2,1)S(1)} %shard_map.128.refs_5_.c0), channel_id=1, source_target_pairs={{0,6},{1,7},{2,4},{3,5},{4,2},{5,3},{6,0},{7,1},{8,14},{9,15},{10,... | collective-permute-start | bytes 110600 | tf_op jit(solution)/shard_map/ppermute | solution.py:387
  6.1 4.9 %collective-permute-start.1 = (bf16[16,1152]{1,0:T(8,128)(2,1)S(1)}, bf16[16,1152]{1,0:T(8,128)(2,1)S(1)}, u32[]{:S(2)}, u32[]{:S(2)}) collective-permute-start(bf16[16,1152]{1,0:T(8,128)(2,1)S(1)} %shard_map.128.refs_5_.c0), channel_id=1, source_target_pairs={{0,4},{1,5},{2,6},{3,7},{4,0},{5,1},{6,2},{7,3},{8,12},{9,13},{10,... | collective-permute-start | bytes 110600 | tf_op jit(solution)/shard_map/ppermute | solution.py:387
  6.1 4.9 %collective-permute-start = (bf16[16,1152]{1,0:T(8,128)(2,1)S(1)}, bf16[16,1152]{1,0:T(8,128)(2,1)S(1)}, u32[]{:S(2)}, u32[]{:S(2)}) collective-permute-start(bf16[16,1152]{1,0:T(8,128)(2,1)S(1)} %shard_map.128.refs_5_.c0), channel_id=1, source_target_pairs={{0,2},{1,3},{2,0},{3,1},{4,6},{5,7},{6,4},{7,5},{8,10},{9,11},{10,... | collective-permute-start | bytes 110600 | tf_op jit(solution)/shard_map/ppermute | solution.py:387
  11.0 16.4 %copy-start.1 = (s32[2]{0:T(128)S(1)}, s32[2]{0:T(128)}, u32[]{:S(2)}) copy-start(s32[2]{0:T(128)} %group.1) | copy-start | bytes 28
  11.0 16.4 %copy-start.2 = (s32[4]{0:T(128)S(1)}, s32[4]{0:T(128)}, u32[]{:S(2)}) copy-start(s32[4]{0:T(128)} %prompt_len.1) | copy-start | bytes 52
  11.0 8.5 %collective-permute-start.5 = (bf16[64,1152]{1,0:T(8,128)(2,1)S(1)}, bf16[64,1152]{1,0:T(8,128)(2,1)S(1)}, u32[]{:S(2)}, u32[]{:S(2)}) collective-permute-start(bf16[64,1152]{1,0:T(8,128)(2,1)S(1)} %shard_map.130.refs_5_.o0.near), channel_id=1, source_target_pairs={{0,24},{1,25},{2,26},{3,27},{4,28},{5,29},{6,30},{7,31},{8,16},{9,... | collective-permute-start | bytes 442376 | tf_op jit(solution)/shard_map/ppermute | solution.py:387
  14.1 7.5 %collective-permute-start.4 = (bf16[64,1152]{1,0:T(8,128)(2,1)S(1)}, bf16[64,1152]{1,0:T(8,128)(2,1)S(1)}, u32[]{:S(2)}, u32[]{:S(2)}) collective-permute-start(bf16[64,1152]{1,0:T(8,128)(2,1)S(1)} %shard_map.130.refs_5_.o0.near), channel_id=1, source_target_pairs={{0,16},{1,17},{2,18},{3,19},{4,20},{5,21},{6,22},{7,23},{8,24},{9,... | collective-permute-start | bytes 442376 | tf_op jit(solution)/shard_map/ppermute | solution.py:387
  14.8 6.9 %collective-permute-start.3 = (bf16[64,1152]{1,0:T(8,128)(2,1)S(1)}, bf16[64,1152]{1,0:T(8,128)(2,1)S(1)}, u32[]{:S(2)}, u32[]{:S(2)}) collective-permute-start(bf16[64,1152]{1,0:T(8,128)(2,1)S(1)} %shard_map.130.refs_5_.o0.near), channel_id=1, source_target_pairs={{0,8},{1,9},{2,10},{3,11},{4,12},{5,13},{6,14},{7,15},{8,0},{9,1},... | collective-permute-start | bytes 442376 | tf_op jit(solution)/shard_map/ppermute | solution.py:387
  15.2 7.0 %collective-permute-start.6 = (bf16[64,1152]{1,0:T(8,128)(2,1)S(1)}, bf16[64,1152]{1,0:T(8,128)(2,1)S(1)}, u32[]{:S(2)}, u32[]{:S(2)}) collective-permute-start(bf16[64,1152]{1,0:T(8,128)(2,1)S(1)} %shard_map.130.refs_5_.o0.near), channel_id=1, source_target_pairs={{0,1},{1,0},{2,3},{3,2},{4,5},{5,4},{6,7},{7,6},{8,9},{9,8},{10,11... | collective-permute-start | bytes 442376 | tf_op jit(solution)/shard_map/ppermute | solution.py:387
  19.5 2.7 %collective-permute-start.9 = (bf16[64,1152]{1,0:T(8,128)(2,1)S(1)}, bf16[64,1152]{1,0:T(8,128)(2,1)S(1)}, u32[]{:S(2)}, u32[]{:S(2)}) collective-permute-start(bf16[64,1152]{1,0:T(8,128)(2,1)S(1)} %collective-permute-done.5.o3), channel_id=1, source_target_pairs={{0,1},{1,0},{2,3},{3,2},{4,5},{5,4},{6,7},{7,6},{8,9},{9,8},{10,11... | collective-permute-start | bytes 442376 | tf_op jit(solution)/shard_map/ppermute | solution.py:387
  21.6 1.4 %collective-permute-start.8 = (bf16[64,1152]{1,0:T(8,128)(2,1)S(1)}, bf16[64,1152]{1,0:T(8,128)(2,1)S(1)}, u32[]{:S(2)}, u32[]{:S(2)}) collective-permute-start(bf16[64,1152]{1,0:T(8,128)(2,1)S(1)} %collective-permute-done.4.o2), channel_id=1, source_target_pairs={{0,1},{1,0},{2,3},{3,2},{4,5},{5,4},{6,7},{7,6},{8,9},{9,8},{10,11... | collective-permute-start | bytes 442376 | tf_op jit(solution)/shard_map/ppermute | solution.py:387
  21.6 1.6 %collective-permute-start.7 = (bf16[64,1152]{1,0:T(8,128)(2,1)S(1)}, bf16[64,1152]{1,0:T(8,128)(2,1)S(1)}, u32[]{:S(2)}, u32[]{:S(2)}) collective-permute-start(bf16[64,1152]{1,0:T(8,128)(2,1)S(1)} %shard_map.132.o1), channel_id=1, source_target_pairs={{0,1},{1,0},{2,3},{3,2},{4,5},{5,4},{6,7},{7,6},{8,9},{9,8},{10,11... | collective-permute-start | bytes 442376 | tf_op jit(solution)/shard_map/ppermute | solution.py:387
  23.3 9.5 %collective-permute-start.12 = (f32[8,128]{1,0:T(8,128)S(1)}, f32[8,128]{1,0:T(8,128)S(1)}, u32[]{:S(2)}, u32[]{:S(2)}) collective-permute-start(f32[8,128]{1,0:T(8,128)S(1)} %shard_map.133.after), channel_id=1, source_target_pairs={{0,192},{32,224},{64,128},{96,160},{128,64},{160,96},{192,0},{224,... | collective-permute-start | bytes 12296 | tf_op jit(solution)/shard_map/ppermute | solution.py:387
  23.9 8.9 %collective-permute-start.11 = (f32[8,128]{1,0:T(8,128)S(1)}, f32[8,128]{1,0:T(8,128)S(1)}, u32[]{:S(2)}, u32[]{:S(2)}) collective-permute-start(f32[8,128]{1,0:T(8,128)S(1)} %shard_map.133.after), channel_id=1, source_target_pairs={{0,128},{32,160},{64,192},{96,224},{128,0},{160,32},{192,64},{224,... | collective-permute-start | bytes 12296 | tf_op jit(solution)/shard_map/ppermute | solution.py:387
  26.6 6.2 %collective-permute-start.10 = (f32[8,128]{1,0:T(8,128)S(1)}, f32[8,128]{1,0:T(8,128)S(1)}, u32[]{:S(2)}, u32[]{:S(2)}) collective-permute-start(f32[8,128]{1,0:T(8,128)S(1)} %shard_map.133.after), channel_id=1, source_target_pairs={{0,64},{32,96},{64,0},{96,32},{128,192},{160,224},{192,128},{224,1... | collective-permute-start | bytes 12296 | tf_op jit(solution)/shard_map/ppermute | solution.py:387
  32.7 11.6 %copy-start = (bf16[256,512]{1,0:T(8,128)(2,1)S(1)}, bf16[256,512]{1,0:T(8,128)(2,1)}, u32[]{:S(2)}) copy-start(bf16[256,512]{1,0:T(8,128)(2,1)} %kown.1) | copy-start | bytes 786436
  32.8 2.0 %collective-permute-start.13 = (f32[2,64,1024]{2,1,0:T(8,128)S(1)}, f32[2,64,1024]{2,1,0:T(8,128)S(1)}, u32[]{:S(2)}, u32[]{:S(2)}) collective-permute-start(f32[2,64,1024]{2,1,0:T(8,128)S(1)} %shard_map.135), channel_id=1, source_target_pairs={{0,1},{1,0},{2,3},{3,2},{4,5},{5,4},{6,7},{7,6},{8,9},{9,8},{10,11... | collective-permute-start | bytes 1572872 | tf_op jit(solution)/shard_map/ppermute | solution.py:387
  34.9 12.2 %collective-permute-start.15 = (bf16[2,16,1024]{2,1,0:T(8,128)(2,1)S(1)}, bf16[2,16,1024]{2,1,0:T(8,128)(2,1)S(1)}, u32[]{:S(2)}, u32[]{:S(2)}) collective-permute-start(bf16[2,16,1024]{2,1,0:T(8,128)(2,1)S(1)} %get-tuple-element.59), channel_id=1, source_target_pairs={{0,6},{1,7},{2,4},{3,5},{4,2},{5,3},{6,0},{7,1},{8,14},{9,15},{10,... | collective-permute-start | bytes 196616 | tf_op jit(solution)/shard_map/ppermute | solution.py:387
  37.4 9.7 %collective-permute-start.16 = (bf16[2,16,1024]{2,1,0:T(8,128)(2,1)S(1)}, bf16[2,16,1024]{2,1,0:T(8,128)(2,1)S(1)}, u32[]{:S(2)}, u32[]{:S(2)}) collective-permute-start(bf16[2,16,1024]{2,1,0:T(8,128)(2,1)S(1)} %get-tuple-element.60), channel_id=1, source_target_pairs={{0,4},{1,5},{2,6},{3,7},{4,0},{5,1},{6,2},{7,3},{8,12},{9,13},{10,... | collective-permute-start | bytes 196616 | tf_op jit(solution)/shard_map/ppermute | solution.py:387
  37.4 9.7 %collective-permute-start.17 = (bf16[2,16,1024]{2,1,0:T(8,128)(2,1)S(1)}, bf16[2,16,1024]{2,1,0:T(8,128)(2,1)S(1)}, u32[]{:S(2)}, u32[]{:S(2)}) collective-permute-start(bf16[2,16,1024]{2,1,0:T(8,128)(2,1)S(1)} %get-tuple-element.61), channel_id=1, source_target_pairs={{0,2},{1,3},{2,0},{3,1},{4,6},{5,7},{6,4},{7,5},{8,10},{9,11},{10,... | collective-permute-start | bytes 196616 | tf_op jit(solution)/shard_map/ppermute | solution.py:387
  39.4 7.7 %collective-permute-start.14 = (f32[8,128]{1,0:T(8,128)S(1)}, f32[8,128]{1,0:T(8,128)S(1)}, u32[]{:S(2)}, u32[]{:S(2)}) collective-permute-start(f32[8,128]{1,0:T(8,128)S(1)} %shard_map.137), channel_id=1, source_target_pairs={{0,32},{32,0},{64,96},{96,64},{128,160},{160,128},{192,224},{224,1... | collective-permute-start | bytes 12296 | tf_op jit(solution)/shard_map/ppermute | solution.py:387
  47.2 5.5 %collective-permute-start.18 = (bf16[16,1024]{1,0:T(8,128)(2,1)S(1)}, bf16[16,1024]{1,0:T(8,128)(2,1)S(1)}, u32[]{:S(2)}, u32[]{:S(2)}) collective-permute-start(bf16[16,1024]{1,0:T(8,128)(2,1)S(1)} %get-tuple-element.66), channel_id=1, source_target_pairs={{0,16},{1,17},{2,18},{3,19},{4,20},{5,21},{6,22},{7,23},{8,24},{9,... | collective-permute-start | bytes 98312 | tf_op jit(solution)/shard_map/ppermute | solution.py:387
  49.4 5.1 %collective-permute-start.19 = (bf16[16,1024]{1,0:T(8,128)(2,1)S(1)}, bf16[16,1024]{1,0:T(8,128)(2,1)S(1)}, u32[]{:S(2)}, u32[]{:S(2)}) collective-permute-start(bf16[16,1024]{1,0:T(8,128)(2,1)S(1)} %get-tuple-element.67), channel_id=1, source_target_pairs={{0,24},{1,25},{2,26},{3,27},{4,28},{5,29},{6,30},{7,31},{8,16},{9,... | collective-permute-start | bytes 98312 | tf_op jit(solution)/shard_map/ppermute | solution.py:387
  50.4 4.1 %collective-permute-start.20 = (bf16[16,1024]{1,0:T(8,128)(2,1)S(1)}, bf16[16,1024]{1,0:T(8,128)(2,1)S(1)}, u32[]{:S(2)}, u32[]{:S(2)}) collective-permute-start(bf16[16,1024]{1,0:T(8,128)(2,1)S(1)} %get-tuple-element.68), channel_id=1, source_target_pairs={{0,8},{1,9},{2,10},{3,11},{4,12},{5,13},{6,14},{7,15},{8,0},{9,1},... | collective-permute-start | bytes 98312 | tf_op jit(solution)/shard_map/ppermute | solution.py:387

commit v4 on v3

--- a/solution.py
+++ b/solution.py
@@ -427,7 +427,7 @@
         sum_kernel, "vvvvvvaa", [near[0], far[0], k0, *got, own, count],
         [((16, wide), F32)] + [((16, wide), BF16)] * 3,
     )
-    got = [swap(s, 8 * m) for m, s in ((2, s2), (3, s3), (1, s1))]
+    got = [swap(s, 8 * m) for m, s in ((3, s3), (2, s2), (1, s1))]
     query_grad, comp_key_grad, comp_value_grad = scale_part(count, dq, own, k1)
     prompt_key_grad, prompt_value_grad = call(
         last_kernel, "vvvvv", [count, k1, *got], [((16, KVW), BF16)] * 2

time: 55.4 us -> 55.5 us (level)
    ppermute x21, starting transfers between devices: 27.4 us -> 27.9 us  [swap(): lax.ppermute(x, axis, [(i, i ^ mask) for i in range(lax.axis_size(axis))])]
  transfers between devices with their start and end apart: 21 -> 21, of which waited for: 8 -> 7; matrix products, arithmetic and copies ran while one was open for 0% -> 0% of each run, Pallas kernels for 27% -> 27%
where the time goes in v4:
time: 55.5 us; the launch traced here: 55.3 us
  starting transfers between devices  27.9 us (50%)
  Pallas kernels  16.8 us (30%)
  waiting for transfers between devices  9.67 us (17%)
  between operations  0.83 us (1%)
    ppermute x21, starting transfers between devices, swap(): lax.ppermute(x, axis, [(i, i ^ mask) for i in range(lax.axis_size(axis))])  27.9 us
    pallas_call x11, Pallas kernels, call(): pl.pallas_call(kernel, out_shape=[jax.ShapeDtypeStruct(s, d) for s, d in...  16.8 us
    ppermute x21, waiting for transfers between devices, swap(): lax.ppermute(x, axis, [(i, i ^ mask) for i in range(lax.axis_size(axis))])  9.67 us
  transfers between devices with their start and end apart: 21, of which 7 were waited for; matrix products, arithmetic and copies ran while one was open for 0% of the time, Pallas kernels for 27%

profile of v4, /device:TPU:4, one launch (start us, length us, event | category | flops | bytes accessed | tf_op | source)
XLA Modules:
  0.0 55.3 jit_solution(7419416062657745985)
XLA Ops:
  0.6 0.8 %shard_map.128.refs_5_.c0 = bf16[16,1152]{1,0:T(8,128)(2,1)S(1)} custom-call(s32[2]{0:T(128)} %refs_0_.3, s32[2]{0:T(128)} %group.1, bf16[16,512]{1,0:T(8,128)(2,1)} %prompt_key.1, bf16[16,512]{1,0:T(8,128)(2,1)} %prompt_value.1), custom_call_target="tpu_custom_call" | custom-call | flops 1 | bytes 1 | tf_op jit(solution)/shard_map/pallas_call | solution.py:311
  1.4 4.7 %collective-permute-start.2 = (bf16[16,1152]{1,0:T(8,128)(2,1)S(1)}, bf16[16,1152]{1,0:T(8,128)(2,1)S(1)}, u32[]{:S(2)}, u32[]{:S(2)}) collective-permute-start(bf16[16,1152]{1,0:T(8,128)(2,1)S(1)} %shard_map.128.refs_5_.c0), channel_id=1, source_target_pairs={{0,6},{1,7},{2,4},{3,5},{4,2},{5,3},{6,0},{7,1},{8,14},{9,15},{10,... | collective-permute-start | bytes 110600 | tf_op jit(solution)/shard_map/ppermute | solution.py:387
  6.1 0.0 collective-permute-start.1
  6.1 0.7 %collective-permute-start = (bf16[16,1152]{1,0:T(8,128)(2,1)S(1)}, bf16[16,1152]{1,0:T(8,128)(2,1)S(1)}, u32[]{:S(2)}, u32[]{:S(2)}) collective-permute-start(bf16[16,1152]{1,0:T(8,128)(2,1)S(1)} %shard_map.128.refs_5_.c0), channel_id=1, source_target_pairs={{0,2},{1,3},{2,0},{3,1},{4,6},{5,7},{6,4},{7,5},{8,10},{9,11},{10,... | collective-permute-start | bytes 110600 | tf_op jit(solution)/shard_map/ppermute | solution.py:387
  6.8 2.7 %shard_map.129 = (bf16[128,4096]{1,0:T(8,128)(2,1)S(1)}, bf16[128,4096]{1,0:T(8,128)(2,1)S(1)}, f32[4,128,1024]{2,1,0:T(8,128)S(1)}, f32[4,128,1024]{2,1,0:T(8,128)S(1)}, f32[8,1024]{1,0:T(8,128)S(1)}) custom-call(s32[2]{0:T(128)} %refs_0_.3, bf16[256,4096]{1,0:T(8,128)(2,1)} %refs_1_.3, bf16[256,4096]{1,0:T(8,128)(2,1)} %refs_2_.3, bf16[256,512]{1,0:T(8,128)(2,1)} %kown.1, ...), custom_call_target="tpu_custom_call" | custom-call | flops 1 | bytes 1 | tf_op jit(solution)/shard_map/pallas_call | solution.py:311
  9.5 0.0 collective-permute-done.2.c3
  9.6 1.4 %collective-permute-done.1.c2 = bf16[16,1152]{1,0:T(8,128)(2,1)S(1)} collective-permute-done((bf16[16,1152]{1,0:T(8,128)(2,1)S(1)}, bf16[16,1152]{1,0:T(8,128)(2,1)S(1)}, u32[]{:S(2)}, u32[]{:S(2)}) %collective-permute-start.1) | collective-permute-done | bytes 36896 | tf_op jit(solution)/shard_map/ppermute | solution.py:387
  11.0 0.0 collective-permute-done.c1
  11.0 0.0 copy-start.1
  11.0 0.0 copy-start.2
  11.0 3.1 %collective-permute-start.5 = (bf16[64,1152]{1,0:T(8,128)(2,1)S(1)}, bf16[64,1152]{1,0:T(8,128)(2,1)S(1)}, u32[]{:S(2)}, u32[]{:S(2)}) collective-permute-start(bf16[64,1152]{1,0:T(8,128)(2,1)S(1)} %shard_map.130.refs_5_.o0.near), channel_id=1, source_target_pairs={{0,24},{1,25},{2,26},{3,27},{4,28},{5,29},{6,30},{7,31},{8,16},{9,... | collective-permute-start | bytes 442376 | tf_op jit(solution)/shard_map/ppermute | solution.py:387
  14.1 0.6 %collective-permute-start.4 = (bf16[64,1152]{1,0:T(8,128)(2,1)S(1)}, bf16[64,1152]{1,0:T(8,128)(2,1)S(1)}, u32[]{:S(2)}, u32[]{:S(2)}) collective-permute-start(bf16[64,1152]{1,0:T(8,128)(2,1)S(1)} %shard_map.130.refs_5_.o0.near), channel_id=1, source_target_pairs={{0,16},{1,17},{2,18},{3,19},{4,20},{5,21},{6,22},{7,23},{8,24},{9,... | collective-permute-start | bytes 442376 | tf_op jit(solution)/shard_map/ppermute | solution.py:387
  14.8 0.5 collective-permute-start.3
  15.2 0.0 collective-permute-start.6
  15.2 2.7 %shard_map.131 = (bf16[128,4096]{1,0:T(8,128)(2,1)S(1)}, bf16[128,4096]{1,0:T(8,128)(2,1)S(1)}, f32[4,128,1024]{2,1,0:T(8,128)S(1)}, f32[4,128,1024]{2,1,0:T(8,128)S(1)}, f32[8,1024]{1,0:T(8,128)S(1)}) custom-call(s32[2]{0:T(128)} %refs_0_.3, bf16[256,4096]{1,0:T(8,128)(2,1)} %refs_1_.3, bf16[256,4096]{1,0:T(8,128)(2,1)} %refs_2_.3, bf16[256,512]{1,0:T(8,128)(2,1)} %kown.1, ...), custom_call_target="tpu_custom_call" | custom-call | flops 1 | bytes 1 | tf_op jit(solution)/shard_map/pallas_call | solution.py:311
  18.0 1.5 %collective-permute-done.5.o3 = bf16[64,1152]{1,0:T(8,128)(2,1)S(1)} collective-permute-done((bf16[64,1152]{1,0:T(8,128)(2,1)S(1)}, bf16[64,1152]{1,0:T(8,128)(2,1)S(1)}, u32[]{:S(2)}, u32[]{:S(2)}) %collective-permute-start.5) | collective-permute-done | bytes 147488 | tf_op jit(solution)/shard_map/ppermute | solution.py:387
  19.5 0.0 collective-permute-start.9
  19.5 2.1 %collective-permute-done.4.o2 = bf16[64,1152]{1,0:T(8,128)(2,1)S(1)} collective-permute-done((bf16[64,1152]{1,0:T(8,128)(2,1)S(1)}, bf16[64,1152]{1,0:T(8,128)(2,1)S(1)}, u32[]{:S(2)}, u32[]{:S(2)}) %collective-permute-start.4) | collective-permute-done | bytes 147488 | tf_op jit(solution)/shard_map/ppermute | solution.py:387
  21.6 0.0 collective-permute-start.8
  21.6 0.0 collective-permute-done.3.refs_0_
  21.6 0.5 collective-permute-start.7
  22.2 0.0 collective-permute-done.6.t0.far
  22.2 0.0 collective-permute-done.9.t3
  22.2 0.8 %collective-permute-done.8.t2 = bf16[64,1152]{1,0:T(8,128)(2,1)S(1)} collective-permute-done((bf16[64,1152]{1,0:T(8,128)(2,1)S(1)}, bf16[64,1152]{1,0:T(8,128)(2,1)S(1)}, u32[]{:S(2)}, u32[]{:S(2)}) %collective-permute-start.8) | collective-permute-done | bytes 147488 | tf_op jit(solution)/shard_map/ppermute | solution.py:387
  23.0 0.2 collective-permute-done.7.t1
  23.3 0.6 %collective-permute-start.12 = (f32[8,128]{1,0:T(8,128)S(1)}, f32[8,128]{1,0:T(8,128)S(1)}, u32[]{:S(2)}, u32[]{:S(2)}) collective-permute-start(f32[8,128]{1,0:T(8,128)S(1)} %shard_map.133.after), channel_id=1, source_target_pairs={{0,192},{32,224},{64,128},{96,160},{128,64},{160,96},{192,0},{224,... | collective-permute-start | bytes 12296 | tf_op jit(solution)/shard_map/ppermute | solution.py:387
  23.9 2.7 %collective-permute-start.11 = (f32[8,128]{1,0:T(8,128)S(1)}, f32[8,128]{1,0:T(8,128)S(1)}, u32[]{:S(2)}, u32[]{:S(2)}) collective-permute-start(f32[8,128]{1,0:T(8,128)S(1)} %shard_map.133.after), channel_id=1, source_target_pairs={{0,128},{32,160},{64,192},{96,224},{128,0},{160,32},{192,64},{224,... | collective-permute-start | bytes 12296 | tf_op jit(solution)/shard_map/ppermute | solution.py:387
  26.6 0.8 %collective-permute-start.10 = (f32[8,128]{1,0:T(8,128)S(1)}, f32[8,128]{1,0:T(8,128)S(1)}, u32[]{:S(2)}, u32[]{:S(2)}) collective-permute-start(f32[8,128]{1,0:T(8,128)S(1)} %shard_map.133.after), channel_id=1, source_target_pairs={{0,64},{32,96},{64,0},{96,32},{128,192},{160,224},{192,128},{224,1... | collective-permute-start | bytes 12296 | tf_op jit(solution)/shard_map/ppermute | solution.py:387
  27.4 0.0 copy-done.1
  27.4 0.0 copy-done.2
  27.4 5.3 %shard_map.134 = (bf16[4,128,1024]{2,1,0:T(8,128)(2,1)S(1)}, f32[8,1024]{1,0:T(8,128)S(1)}, bf16[128,512]{1,0:T(8,128)(2,1)S(1)}, bf16[4,128,1024]{2,1,0:T(8,128...) custom-call(s32[2]{0:T(128)S(1)} %copy-done.1, ...), custom_call_target="tpu_custom_call" | custom-call | flops 1 | bytes 1 | tf_op jit(solution)/shard_map/pallas_call | solution.py:311
  32.7 0.0 copy-start
  32.8 0.0 collective-permute-done.12
  32.8 0.0 collective-permute-done.11
  32.8 0.0 collective-permute-done.10
  32.8 0.1 collective-permute-start.13
  32.9 1.9 %collective-permute-done.13.got = f32[2,64,1024]{2,1,0:T(8,128)S(1)} collective-permute-done((f32[2,64,1024]{2,1,0:T(8,128)S(1)}, f32[2,64,1024]{2,1,0:T(8,128)S(1)}, u32[]{:S(2)}, u32[]{:S(2)}) %collective-permute-start.13) | collective-permute-done | bytes 524320 | tf_op jit(solution)/shard_map/ppermute | solution.py:387
  34.8 0.1 shard_map.136
  34.9 2.5 %collective-permute-start.15 = (bf16[2,16,1024]{2,1,0:T(8,128)(2,1)S(1)}, bf16[2,16,1024]{2,1,0:T(8,128)(2,1)S(1)}, u32[]{:S(2)}, u32[]{:S(2)}) collective-permute-start(bf16[2,16,1024]{2,1,0:T(8,128)(2,1)S(1)} %get-tuple-element.59), channel_id=1, source_target_pairs={{0,6},{1,7},{2,4},{3,5},{4,2},{5,3},{6,0},{7,1},{8,14},{9,15},{10,... | collective-permute-start | bytes 196616 | tf_op jit(solution)/shard_map/ppermute | solution.py:387
  37.4 0.0 collective-permute-start.16
  37.4 2.0 %collective-permute-start.17 = (bf16[2,16,1024]{2,1,0:T(8,128)(2,1)S(1)}, bf16[2,16,1024]{2,1,0:T(8,128)(2,1)S(1)}, u32[]{:S(2)}, u32[]{:S(2)}) collective-permute-start(bf16[2,16,1024]{2,1,0:T(8,128)(2,1)S(1)} %get-tuple-element.61), channel_id=1, source_target_pairs={{0,2},{1,3},{2,0},{3,1},{4,6},{5,7},{6,4},{7,5},{8,10},{9,11},{10,... | collective-permute-start | bytes 196616 | tf_op jit(solution)/shard_map/ppermute | solution.py:387
  39.4 4.9 %collective-permute-start.14 = (f32[8,128]{1,0:T(8,128)S(1)}, f32[8,128]{1,0:T(8,128)S(1)}, u32[]{:S(2)}, u32[]{:S(2)}) collective-permute-start(f32[8,128]{1,0:T(8,128)S(1)} %shard_map.137), channel_id=1, source_target_pairs={{0,32},{32,0},{64,96},{96,64},{128,160},{160,128},{192,224},{224,1... | collective-permute-start | bytes 12296 | tf_op jit(solution)/shard_map/ppermute | solution.py:387
  44.3 0.0 copy-done
  44.3 2.7 %shard_map.138 = (f32[256,4096]{1,0:T(8,128)S(1)}, f32[256,1024]{1,0:T(8,128)S(1)}) custom-call(bf16[128,4096]{1,0:T(8,128)(2,1)S(1)} %get-tuple-element.40.q0, bf16[128,4096]{1,0:T(8,128)(2,1)S(1)} %get-tuple-element.41.do0, f32[4,128,1024]{2,1,0:T(8,128)S(1)} %get-tuple-element.42.e0, f32[4,128,1024]{2,1,0:T(8,128)S(1)} %get-tuple-element.43.g0, ...), custom_call_target="tpu_custom_call" | custom-call | flops 1 | bytes 1 | tf_op jit(solution)/shard_map/pallas_call | solution.py:311
  47.0 0.0 collective-permute-done.14
  47.1 0.0 collective-permute-done.15.r1
  47.1 0.0 collective-permute-done.16.r2
  47.1 0.0 collective-permute-done.17.r3
  47.1 0.1 shard_map.139
  47.2 2.0 %collective-permute-start.18 = (bf16[16,1024]{1,0:T(8,128)(2,1)S(1)}, bf16[16,1024]{1,0:T(8,128)(2,1)S(1)}, u32[]{:S(2)}, u32[]{:S(2)}) collective-permute-start(bf16[16,1024]{1,0:T(8,128)(2,1)S(1)} %get-tuple-element.66), channel_id=1, source_target_pairs={{0,24},{1,25},{2,26},{3,27},{4,28},{5,29},{6,30},{7,31},{8,16},{9,... | collective-permute-start | bytes 98312 | tf_op jit(solution)/shard_map/ppermute | solution.py:387
  49.2 0.6 %collective-permute-start.19 = (bf16[16,1024]{1,0:T(8,128)(2,1)S(1)}, bf16[16,1024]{1,0:T(8,128)(2,1)S(1)}, u32[]{:S(2)}, u32[]{:S(2)}) collective-permute-start(bf16[16,1024]{1,0:T(8,128)(2,1)S(1)} %get-tuple-element.67), channel_id=1, source_target_pairs={{0,16},{1,17},{2,18},{3,19},{4,20},{5,21},{6,22},{7,23},{8,24},{9,... | collective-permute-start | bytes 98312 | tf_op jit(solution)/shard_map/ppermute | solution.py:387
  49.8 1.6 %collective-permute-start.20 = (bf16[16,1024]{1,0:T(8,128)(2,1)S(1)}, bf16[16,1024]{1,0:T(8,128)(2,1)S(1)}, u32[]{:S(2)}, u32[]{:S(2)}) collective-permute-start(bf16[16,1024]{1,0:T(8,128)(2,1)S(1)} %get-tuple-element.68), channel_id=1, source_target_pairs={{0,8},{1,9},{2,10},{3,11},{4,12},{5,13},{6,14},{7,15},{8,0},{9,1},... | collective-permute-start | bytes 98312 | tf_op jit(solution)/shard_map/ppermute | solution.py:387
  51.4 1.7 %shard_map.140 = (bf16[256,4096]{1,0:T(8,128)(2,1)}, bf16[256,512]{1,0:T(8,128)(2,1)}, bf16[256,512]{1,0:T(8,128)(2,1)}) custom-call(f32[8,128]{1,0:T(8,128)S(1)} %add.15.also.total, f32[256,4096]{1,0:T(8,128)S(1)} %get-tuple-element.57.dq, f32[256,1024]{1,0:T(8,128)S(1)} %get-tuple-element.58.after.own, f32[16,1024]{1,0:T(8,128)S(1)} %get-tuple-element.62.after.k1), custom_call_target="tpu_custom_call" | custom-call | flops 1 | bytes 1 | tf_op jit(solution)/shard_map/pallas_call | solution.py:311
  53.1 0.0 collective-permute-done.18.r1
  53.1 1.6 %collective-permute-done.19.r2 = bf16[16,1024]{1,0:T(8,128)(2,1)S(1)} collective-permute-done((bf16[16,1024]{1,0:T(8,128)(2,1)S(1)}, bf16[16,1024]{1,0:T(8,128)(2,1)S(1)}, u32[]{:S(2)}, u32[]{:S(2)}) %collective-permute-start.19) | collective-permute-done | bytes 32800 | tf_op jit(solution)/shard_map/ppermute | solution.py:387
  54.6 0.0 collective-permute-done.20.r3
  54.6 0.7 %shard_map.141 = (bf16[16,512]{1,0:T(8,128)(2,1)}, bf16[16,512]{1,0:T(8,128)(2,1)}) custom-call(f32[8,128]{1,0:T(8,128)S(1)} %add.15.also.total, f32[16,1024]{1,0:T(8,128)S(1)} %get-tuple-element.62.after.k1, bf16[16,1024]{1,0:T(8,128)(2,1)S(1)} %collective-permute-done.18.r1, bf16[16,1024]{1,0:T(8,128)(2,1)S(1)} %collective-permute-done.19.r2, ...), custom_call_target="tpu_custom_call" | custom-call | flops 1 | bytes 1 | tf_op jit(solution)/shard_map/pallas_call | solution.py:311
  (7 shorter events, 0.1 us)
Async XLA Ops:
  1.4 8.1 %collective-permute-start.2 = (bf16[16,1152]{1,0:T(8,128)(2,1)S(1)}, bf16[16,1152]{1,0:T(8,128)(2,1)S(1)}, u32[]{:S(2)}, u32[]{:S(2)}) collective-permute-start(bf16[16,1152]{1,0:T(8,128)(2,1)S(1)} %shard_map.128.refs_5_.c0), channel_id=1, source_target_pairs={{0,6},{1,7},{2,4},{3,5},{4,2},{5,3},{6,0},{7,1},{8,14},{9,15},{10,... | collective-permute-start | bytes 110600 | tf_op jit(solution)/shard_map/ppermute | solution.py:387
  6.1 4.9 %collective-permute-start.1 = (bf16[16,1152]{1,0:T(8,128)(2,1)S(1)}, bf16[16,1152]{1,0:T(8,128)(2,1)S(1)}, u32[]{:S(2)}, u32[]{:S(2)}) collective-permute-start(bf16[16,1152]{1,0:T(8,128)(2,1)S(1)} %shard_map.128.refs_5_.c0), channel_id=1, source_target_pairs={{0,4},{1,5},{2,6},{3,7},{4,0},{5,1},{6,2},{7,3},{8,12},{9,13},{10,... | collective-permute-start | bytes 110600 | tf_op jit(solution)/shard_map/ppermute | solution.py:387
  6.1 4.9 %collective-permute-start = (bf16[16,1152]{1,0:T(8,128)(2,1)S(1)}, bf16[16,1152]{1,0:T(8,128)(2,1)S(1)}, u32[]{:S(2)}, u32[]{:S(2)}) collective-permute-start(bf16[16,1152]{1,0:T(8,128)(2,1)S(1)} %shard_map.128.refs_5_.c0), channel_id=1, source_target_pairs={{0,2},{1,3},{2,0},{3,1},{4,6},{5,7},{6,4},{7,5},{8,10},{9,11},{10,... | collective-permute-start | bytes 110600 | tf_op jit(solution)/shard_map/ppermute | solution.py:387
  11.0 16.4 %copy-start.1 = (s32[2]{0:T(128)S(1)}, s32[2]{0:T(128)}, u32[]{:S(2)}) copy-start(s32[2]{0:T(128)} %group.1) | copy-start | bytes 28
  11.0 16.4 %copy-start.2 = (s32[4]{0:T(128)S(1)}, s32[4]{0:T(128)}, u32[]{:S(2)}) copy-start(s32[4]{0:T(128)} %prompt_len.1) | copy-start | bytes 52
  11.0 8.5 %collective-permute-start.5 = (bf16[64,1152]{1,0:T(8,128)(2,1)S(1)}, bf16[64,1152]{1,0:T(8,128)(2,1)S(1)}, u32[]{:S(2)}, u32[]{:S(2)}) collective-permute-start(bf16[64,1152]{1,0:T(8,128)(2,1)S(1)} %shard_map.130.refs_5_.o0.near), channel_id=1, source_target_pairs={{0,24},{1,25},{2,26},{3,27},{4,28},{5,29},{6,30},{7,31},{8,16},{9,... | collective-permute-start | bytes 442376 | tf_op jit(solution)/shard_map/ppermute | solution.py:387
  14.1 7.5 %collective-permute-start.4 = (bf16[64,1152]{1,0:T(8,128)(2,1)S(1)}, bf16[64,1152]{1,0:T(8,128)(2,1)S(1)}, u32[]{:S(2)}, u32[]{:S(2)}) collective-permute-start(bf16[64,1152]{1,0:T(8,128)(2,1)S(1)} %shard_map.130.refs_5_.o0.near), channel_id=1, source_target_pairs={{0,16},{1,17},{2,18},{3,19},{4,20},{5,21},{6,22},{7,23},{8,24},{9,... | collective-permute-start | bytes 442376 | tf_op jit(solution)/shard_map/ppermute | solution.py:387
  14.8 6.9 %collective-permute-start.3 = (bf16[64,1152]{1,0:T(8,128)(2,1)S(1)}, bf16[64,1152]{1,0:T(8,128)(2,1)S(1)}, u32[]{:S(2)}, u32[]{:S(2)}) collective-permute-start(bf16[64,1152]{1,0:T(8,128)(2,1)S(1)} %shard_map.130.refs_5_.o0.near), channel_id=1, source_target_pairs={{0,8},{1,9},{2,10},{3,11},{4,12},{5,13},{6,14},{7,15},{8,0},{9,1},... | collective-permute-start | bytes 442376 | tf_op jit(solution)/shard_map/ppermute | solution.py:387
  15.2 7.0 %collective-permute-start.6 = (bf16[64,1152]{1,0:T(8,128)(2,1)S(1)}, bf16[64,1152]{1,0:T(8,128)(2,1)S(1)}, u32[]{:S(2)}, u32[]{:S(2)}) collective-permute-start(bf16[64,1152]{1,0:T(8,128)(2,1)S(1)} %shard_map.130.refs_5_.o0.near), channel_id=1, source_target_pairs={{0,1},{1,0},{2,3},{3,2},{4,5},{5,4},{6,7},{7,6},{8,9},{9,8},{10,11... | collective-permute-start | bytes 442376 | tf_op jit(solution)/shard_map/ppermute | solution.py:387
  19.5 2.7 %collective-permute-start.9 = (bf16[64,1152]{1,0:T(8,128)(2,1)S(1)}, bf16[64,1152]{1,0:T(8,128)(2,1)S(1)}, u32[]{:S(2)}, u32[]{:S(2)}) collective-permute-start(bf16[64,1152]{1,0:T(8,128)(2,1)S(1)} %collective-permute-done.5.o3), channel_id=1, source_target_pairs={{0,1},{1,0},{2,3},{3,2},{4,5},{5,4},{6,7},{7,6},{8,9},{9,8},{10,11... | collective-permute-start | bytes 442376 | tf_op jit(solution)/shard_map/ppermute | solution.py:387
  21.6 1.4 %collective-permute-start.8 = (bf16[64,1152]{1,0:T(8,128)(2,1)S(1)}, bf16[64,1152]{1,0:T(8,128)(2,1)S(1)}, u32[]{:S(2)}, u32[]{:S(2)}) collective-permute-start(bf16[64,1152]{1,0:T(8,128)(2,1)S(1)} %collective-permute-done.4.o2), channel_id=1, source_target_pairs={{0,1},{1,0},{2,3},{3,2},{4,5},{5,4},{6,7},{7,6},{8,9},{9,8},{10,11... | collective-permute-start | bytes 442376 | tf_op jit(solution)/shard_map/ppermute | solution.py:387
  21.6 1.6 %collective-permute-start.7 = (bf16[64,1152]{1,0:T(8,128)(2,1)S(1)}, bf16[64,1152]{1,0:T(8,128)(2,1)S(1)}, u32[]{:S(2)}, u32[]{:S(2)}) collective-permute-start(bf16[64,1152]{1,0:T(8,128)(2,1)S(1)} %shard_map.132.o1), channel_id=1, source_target_pairs={{0,1},{1,0},{2,3},{3,2},{4,5},{5,4},{6,7},{7,6},{8,9},{9,8},{10,11... | collective-permute-start | bytes 442376 | tf_op jit(solution)/shard_map/ppermute | solution.py:387
  23.3 9.5 %collective-permute-start.12 = (f32[8,128]{1,0:T(8,128)S(1)}, f32[8,128]{1,0:T(8,128)S(1)}, u32[]{:S(2)}, u32[]{:S(2)}) collective-permute-start(f32[8,128]{1,0:T(8,128)S(1)} %shard_map.133.after), channel_id=1, source_target_pairs={{0,192},{32,224},{64,128},{96,160},{128,64},{160,96},{192,0},{224,... | collective-permute-start | bytes 12296 | tf_op jit(solution)/shard_map/ppermute | solution.py:387
  23.9 8.9 %collective-permute-start.11 = (f32[8,128]{1,0:T(8,128)S(1)}, f32[8,128]{1,0:T(8,128)S(1)}, u32[]{:S(2)}, u32[]{:S(2)}) collective-permute-start(f32[8,128]{1,0:T(8,128)S(1)} %shard_map.133.after), channel_id=1, source_target_pairs={{0,128},{32,160},{64,192},{96,224},{128,0},{160,32},{192,64},{224,... | collective-permute-start | bytes 12296 | tf_op jit(solution)/shard_map/ppermute | solution.py:387
  26.6 6.2 %collective-permute-start.10 = (f32[8,128]{1,0:T(8,128)S(1)}, f32[8,128]{1,0:T(8,128)S(1)}, u32[]{:S(2)}, u32[]{:S(2)}) collective-permute-start(f32[8,128]{1,0:T(8,128)S(1)} %shard_map.133.after), channel_id=1, source_target_pairs={{0,64},{32,96},{64,0},{96,32},{128,192},{160,224},{192,128},{224,1... | collective-permute-start | bytes 12296 | tf_op jit(solution)/shard_map/ppermute | solution.py:387
  32.7 11.6 %copy-start = (bf16[256,512]{1,0:T(8,128)(2,1)S(1)}, bf16[256,512]{1,0:T(8,128)(2,1)}, u32[]{:S(2)}) copy-start(bf16[256,512]{1,0:T(8,128)(2,1)} %kown.1) | copy-start | bytes 786436
  32.8 2.0 %collective-permute-start.13 = (f32[2,64,1024]{2,1,0:T(8,128)S(1)}, f32[2,64,1024]{2,1,0:T(8,128)S(1)}, u32[]{:S(2)}, u32[]{:S(2)}) collective-permute-start(f32[2,64,1024]{2,1,0:T(8,128)S(1)} %shard_map.135), channel_id=1, source_target_pairs={{0,1},{1,0},{2,3},{3,2},{4,5},{5,4},{6,7},{7,6},{8,9},{9,8},{10,11... | collective-permute-start | bytes 1572872 | tf_op jit(solution)/shard_map/ppermute | solution.py:387
  34.9 12.2 %collective-permute-start.15 = (bf16[2,16,1024]{2,1,0:T(8,128)(2,1)S(1)}, bf16[2,16,1024]{2,1,0:T(8,128)(2,1)S(1)}, u32[]{:S(2)}, u32[]{:S(2)}) collective-permute-start(bf16[2,16,1024]{2,1,0:T(8,128)(2,1)S(1)} %get-tuple-element.59), channel_id=1, source_target_pairs={{0,6},{1,7},{2,4},{3,5},{4,2},{5,3},{6,0},{7,1},{8,14},{9,15},{10,... | collective-permute-start | bytes 196616 | tf_op jit(solution)/shard_map/ppermute | solution.py:387
  37.4 9.7 %collective-permute-start.16 = (bf16[2,16,1024]{2,1,0:T(8,128)(2,1)S(1)}, bf16[2,16,1024]{2,1,0:T(8,128)(2,1)S(1)}, u32[]{:S(2)}, u32[]{:S(2)}) collective-permute-start(bf16[2,16,1024]{2,1,0:T(8,128)(2,1)S(1)} %get-tuple-element.60), channel_id=1, source_target_pairs={{0,4},{1,5},{2,6},{3,7},{4,0},{5,1},{6,2},{7,3},{8,12},{9,13},{10,... | collective-permute-start | bytes 196616 | tf_op jit(solution)/shard_map/ppermute | solution.py:387
  37.4 9.7 %collective-permute-start.17 = (bf16[2,16,1024]{2,1,0:T(8,128)(2,1)S(1)}, bf16[2,16,1024]{2,1,0:T(8,128)(2,1)S(1)}, u32[]{:S(2)}, u32[]{:S(2)}) collective-permute-start(bf16[2,16,1024]{2,1,0:T(8,128)(2,1)S(1)} %get-tuple-element.61), channel_id=1, source_target_pairs={{0,2},{1,3},{2,0},{3,1},{4,6},{5,7},{6,4},{7,5},{8,10},{9,11},{10,... | collective-permute-start | bytes 196616 | tf_op jit(solution)/shard_map/ppermute | solution.py:387
  39.4 7.7 %collective-permute-start.14 = (f32[8,128]{1,0:T(8,128)S(1)}, f32[8,128]{1,0:T(8,128)S(1)}, u32[]{:S(2)}, u32[]{:S(2)}) collective-permute-start(f32[8,128]{1,0:T(8,128)S(1)} %shard_map.137), channel_id=1, source_target_pairs={{0,32},{32,0},{64,96},{96,64},{128,160},{160,128},{192,224},{224,1... | collective-permute-start | bytes 12296 | tf_op jit(solution)/shard_map/ppermute | solution.py:387
  47.2 5.9 %collective-permute-start.18 = (bf16[16,1024]{1,0:T(8,128)(2,1)S(1)}, bf16[16,1024]{1,0:T(8,128)(2,1)S(1)}, u32[]{:S(2)}, u32[]{:S(2)}) collective-permute-start(bf16[16,1024]{1,0:T(8,128)(2,1)S(1)} %get-tuple-element.66), channel_id=1, source_target_pairs={{0,24},{1,25},{2,26},{3,27},{4,28},{5,29},{6,30},{7,31},{8,16},{9,... | collective-permute-start | bytes 98312 | tf_op jit(solution)/shard_map/ppermute | solution.py:387
  49.2 5.4 %collective-permute-start.19 = (bf16[16,1024]{1,0:T(8,128)(2,1)S(1)}, bf16[16,1024]{1,0:T(8,128)(2,1)S(1)}, u32[]{:S(2)}, u32[]{:S(2)}) collective-permute-start(bf16[16,1024]{1,0:T(8,128)(2,1)S(1)} %get-tuple-element.67), channel_id=1, source_target_pairs={{0,16},{1,17},{2,18},{3,19},{4,20},{5,21},{6,22},{7,23},{8,24},{9,... | collective-permute-start | bytes 98312 | tf_op jit(solution)/shard_map/ppermute | solution.py:387
  49.8 4.8 %collective-permute-start.20 = (bf16[16,1024]{1,0:T(8,128)(2,1)S(1)}, bf16[16,1024]{1,0:T(8,128)(2,1)S(1)}, u32[]{:S(2)}, u32[]{:S(2)}) collective-permute-start(bf16[16,1024]{1,0:T(8,128)(2,1)S(1)} %get-tuple-element.68), channel_id=1, source_target_pairs={{0,8},{1,9},{2,10},{3,11},{4,12},{5,13},{6,14},{7,15},{8,0},{9,1},... | collective-permute-start | bytes 98312 | tf_op jit(solution)/shard_map/ppermute | solution.py:387
